TPU v7x, 32 devices: a whole 2x2x4 slice. The times are simulated.
32 devices in a mesh: tile: 16 (over z, y, x), nrn: 2 (over core).
Axes of the slice: x: 2, y: 2, z: 4, core: 2. Of those that a mesh axis runs over, the one named last changes fastest.
Arguments:
- movie: bfloat16 [2, 128, 1024, 1024], P('nrn', 'tile'), may hold values from 0.099609375 to 2
- shifts: int32 [2, 128, 2], P('nrn', 'tile'), may hold values from -4 to 4
- footprints: bfloat16 [1536, 16, 128], P('tile'), may hold values from 0.019897461 to 1
- blocks: int32 [1536, 16], P('tile'), may hold values from 0 to 18431, as said below
- traces: float32 [2, 1536, 4], P('nrn', 'tile'), may hold values from 0.1 to 2
- counts: int32 [16], P('tile'), may hold values from 24 to 96, as said below
Outputs:
- new_traces: float32 [2, 1536, 4], P('nrn', 'tile')
- new_footprints: bfloat16 [1536, 16, 128], P('tile')
Inputs may be any that keep to these rules, and one draw needn't show every extreme that they name: Each neuron has a plane z < 29, a block row r < 8 and a block column x < 63; blocks[k, 4 a + 2 d + e] = ((z + a) * 9 + r + d) * 64 + x + e for a in 0..3 and d, e in 0..1, so a neuron covers 2 x 2 blocks on each of 4 planes and reaches at most one block row below its tile's rows. `counts`: some tile is full and some holds 24 live neurons in every draw.
All inputs are finite; a program needn't handle non-finite values.
Results may differ from a plain program's by a relative error of at most 0.00105.
Values may be sent and summed in bfloat16 or wider, within the bound.
A program may use at most 256 MiB of HBM per device.

v0:
```python
import functools

import jax
import jax.numpy as jnp
from jax import lax
from jax.experimental import pallas as pl
from jax.experimental.pallas import tpu as pltpu
from jax.sharding import PartitionSpec as P

Z = 32
PR = 8
PC = 16
VOX = 128
NB = 16
SPAN = 4
LANES = 128
WIN_R = 2 * PR
WIN_C = 2 * PC
EPSILON = 1e-06
MIB = 1 << 20
EXACT = lax.Precision.HIGHEST


def extract_kernel(
    cap, step, tiles, plane, frames, height, width,
    rows_ref, cols_ref, counts_ref, shift_ref, group_ref, movie_ref, out_ref, scr,
):
    frame = pl.program_id(0)

    scr[frame, pl.ds(0, 8), :] = jnp.zeros((8, width + 256), jnp.float32)
    scr[frame, pl.ds(height + 8, 16), :] = jnp.zeros((16, width + 256), jnp.float32)

    @pl.loop(0, height // 32)
    def _(i):
        at = pl.ds(pl.multiple_of(i * 32 + 8, 8), 32)
        scr[frame, at, pl.ds(0, 128)] = jnp.zeros((32, 128), jnp.float32)
        scr[frame, at, pl.ds(width + 128, 128)] = jnp.zeros((32, 128), jnp.float32)
        part = movie_ref[0, pl.ds(pl.multiple_of(i * 32, 32), 32), :]
        scr[frame, at, pl.ds(128, width)] = part.astype(jnp.float32)

    @pl.when(frame == frames - 1)
    def _():
        out_ref[...] = jnp.zeros_like(out_ref)
        lane = lax.broadcasted_iota(jnp.int32, (WIN_R + 8, LANES), 1)
        row = lax.broadcasted_iota(jnp.int32, (WIN_R, LANES), 0)
        first = group_ref[0] * frames
        moves = [
            (shift_ref[2 * (plane * frames + f)], shift_ref[2 * (plane * frames + f) + 1]) for f in range(frames)
        ]

        def one(slot):
            r0 = rows_ref[slot]
            c0 = cols_ref[slot]
            window = jnp.zeros((WIN_R, LANES), jnp.float32)
            for f in range(frames):
                down, right = moves[f]
                top = r0 - down + 8
                left = c0 - right + 128
                m = lax.shift_right_logical(left, 7)
                o = left - m * 128
                k = top & 7
                at = pl.ds(pl.multiple_of(top - k, 8), WIN_R + 8)
                near = scr[f, at, pl.ds(pl.multiple_of(m * 128, 128), 128)]
                far = scr[f, at, pl.ds(pl.multiple_of(m * 128 + 128, 128), 128)]
                place = (first + f) * WIN_C
                both = jnp.where(lane >= o, near, far)
                parts = []
                for i in range(0, WIN_R, 8):
                    part = jnp.where(row[:8] >= k, both[i : i + 8], both[i + 8 : i + 16])
                    part = pltpu.roll(part, (8 - k) & 7, 0)
                    parts.append(pltpu.roll(part, (place - o + 128) & 127, 1))
                both = jnp.concatenate(parts, axis=0)
                window = jnp.where((lane[:WIN_R] >= place) & (lane[:WIN_R] < place + WIN_C), both, window)
            return jnp.where(row + r0 < height, window, 0.0).astype(jnp.bfloat16)

        @pl.loop(0, tiles)
        def _(t):
            def some(i, carry):
                slots = [t * cap + i * step + j for j in range(step)]
                windows = [one(slot) for slot in slots]
                for slot, window in zip(slots, windows):
                    out_ref[slot] = window
                return carry

            lax.fori_loop(0, (counts_ref[t] + step - 1) // step, some, 0)


def extract(movie, shifts, rows, cols, counts, group, cap, step, tiles, plane, frames):
    _, height, width = movie.shape
    smem = pl.BlockSpec(memory_space=pltpu.SMEM)
    return pl.pallas_call(
        functools.partial(extract_kernel, cap, step, tiles, plane, frames, height, width),
        grid=(frames,),
        in_specs=[smem] * 5 + [pl.BlockSpec((1, height, width), lambda f: (plane * frames + f, 0, 0))],
        out_specs=pl.BlockSpec((tiles * cap, WIN_R, LANES), lambda f: (0, 0, 0)),
        out_shape=jax.ShapeDtypeStruct((tiles * cap, WIN_R, LANES), jnp.bfloat16),
        scratch_shapes=[pltpu.VMEM((frames, height + 24, width + 256), jnp.float32)],
        compiler_params=pltpu.CompilerParams(vmem_limit_bytes=56 * MIB),
        name="extract_windows",
    )(rows.reshape(-1), cols.reshape(-1), counts, shifts.reshape(-1), group.reshape(1), movie)


def exchange_kernel(tiles, new_ref, numer_ref, near_ref, other_ref, send_sem, recv_sem):
    t, p = lax.axis_index("tile"), lax.axis_index("nrn")
    q = 1 - p
    has_above, has_below = t > 0, t < tiles - 1
    mesh_id = pl.DeviceIdType.MESH
    barrier = pltpu.get_barrier_semaphore()
    pl.semaphore_signal(barrier, inc=1, device_id=(t, q), device_id_type=mesh_id)

    @pl.when(has_above)
    def _():
        for peer in (p, q):
            pl.semaphore_signal(barrier, inc=1, device_id=(t - 1, peer), device_id_type=mesh_id)

    @pl.when(has_below)
    def _():
        for peer in (p, q):
            pl.semaphore_signal(barrier, inc=1, device_id=(t + 1, peer), device_id_type=mesh_id)

    pl.semaphore_wait(barrier, 1 + 2 * has_above.astype(jnp.int32) + 2 * has_below.astype(jnp.int32))

    def copy(src, dst, i, to):
        return pltpu.make_async_remote_copy(
            src_ref=src, dst_ref=dst, send_sem=send_sem.at[i], recv_sem=recv_sem.at[i],
            device_id=to, device_id_type=mesh_id,
        )

    partner = copy(new_ref, near_ref.at[0], 0, (t, q))
    large = copy(numer_ref, other_ref, 5, (t, q))
    to_below = [copy(new_ref, near_ref.at[1 + i], 1 + i, (t + 1, peer)) for i, peer in enumerate((p, q))]
    to_above = [copy(new_ref, near_ref.at[3 + i], 3 + i, (t - 1, peer)) for i, peer in enumerate((p, q))]

    @pl.when(has_below)
    def _():
        for one in to_below:
            one.start()

    @pl.when(has_above)
    def _():
        for one in to_above:
            one.start()

    partner.start()
    large.start()

    @pl.when(has_below)
    def _():
        for one in to_below:
            one.wait_send()
        for one in to_above:
            one.wait_recv()

    @pl.when(has_above)
    def _():
        for one in to_above:
            one.wait_send()
        for one in to_below:
            one.wait_recv()

    partner.wait()
    large.wait()


def exchange(new, numer, tiles):
    anywhere = pl.BlockSpec(memory_space=pl.ANY)
    return pl.pallas_call(
        functools.partial(exchange_kernel, tiles),
        in_specs=[anywhere, anywhere],
        out_specs=[anywhere, anywhere],
        out_shape=[
            jax.ShapeDtypeStruct((5,) + new.shape, jnp.float32),
            jax.ShapeDtypeStruct(numer.shape, jnp.float32),
        ],
        scratch_shapes=[pltpu.SemaphoreType.DMA((6,)), pltpu.SemaphoreType.DMA((6,))],
        compiler_params=pltpu.CompilerParams(collective_id=0, has_side_effects=True),
        name="exchange",
    )(new, numer)


def overlap_kernel(own_ref, own_ids_ref, cols_ref, col_ids_ref, traces_ref, out_ref, acc):
    b = pl.program_id(0)
    products = lax.dot_general(
        own_ref[...], cols_ref[...], (((1,), (1,)), ((), ())), preferred_element_type=jnp.float32
    )
    kept = jnp.where(own_ids_ref[0] == col_ids_ref[...], products, 0.0)

    @pl.when(b == 0)
    def _():
        acc[...] = kept

    @pl.when(b > 0)
    def _():
        acc[...] += kept

    @pl.when(b == pl.num_programs(0) - 1)
    def _():
        out_ref[...] = (
            jnp.dot(acc[...], traces_ref[...], precision=EXACT, preferred_element_type=jnp.float32) + EPSILON
        )


def whole_spec(shape):
    return pl.BlockSpec(shape, lambda i: (0,) * len(shape))


def overlaps(own, own_ids, cols, col_ids, col_traces):
    slots = own.shape[0]
    width = cols.shape[0]
    return pl.pallas_call(
        overlap_kernel,
        grid=(NB,),
        in_specs=[
            pl.BlockSpec((slots, VOX), lambda b: (0, b)),
            pl.BlockSpec((1, slots, 1), lambda b: (b, 0, 0)),
            whole_spec(cols.shape),
            whole_spec(col_ids.shape),
            whole_spec(col_traces.shape),
        ],
        out_specs=whole_spec((slots, LANES)),
        out_shape=jax.ShapeDtypeStruct((slots, LANES), jnp.float32),
        scratch_shapes=[pltpu.VMEM((slots, width), jnp.float32)],
        compiler_params=pltpu.CompilerParams(vmem_limit_bytes=32 * MIB),
        name="denom_c",
    )(own, own_ids, cols, col_ids, col_traces)


def update_kernel(picked_ref, masked_ref, traces_ref, denom_ref, new_ref, numer_ref):
    pairs = masked_ref.shape[0]
    slots = traces_ref.shape[0]
    keep_lane = lax.broadcasted_iota(jnp.int32, (pairs, PR, 2 * VOX), 2)
    keep_row = lax.broadcasted_iota(jnp.int32, (pairs, PR, 2 * VOX), 1)
    keep = (keep_lane & (VOX - 1)) // PC == keep_row
    out_lane = lax.broadcasted_iota(jnp.int32, (LANES, 2 * VOX), 1)
    in_lane = lax.broadcasted_iota(jnp.int32, (LANES, 2 * VOX), 0)
    fold = ((in_lane & (WIN_C - 1)) == (out_lane // VOX) * PC + (out_lane & (PC - 1))).astype(jnp.bfloat16)
    group_a = lax.broadcasted_iota(jnp.int32, (LANES, LANES), 0) // WIN_C
    group_b = lax.broadcasted_iota(jnp.int32, (LANES, LANES), 1) // WIN_C
    group_sum = (group_a == group_b).astype(jnp.float32)

    feet = masked_ref[...].astype(jnp.float32)
    feet = jnp.where(keep, feet[:, None, :], 0.0).reshape(pairs * PR, 2 * VOX).astype(jnp.bfloat16)
    feet = lax.dot_general(feet, fold, (((1,), (1,)), ((), ())), preferred_element_type=jnp.float32)
    seen = picked_ref[...].astype(jnp.float32)
    sums = (feet * seen).reshape(slots, SPAN * WIN_R, LANES).sum(axis=1)
    numer_c = jnp.dot(sums, group_sum, precision=EXACT, preferred_element_type=jnp.float32)
    new = traces_ref[...] * numer_c / denom_ref[...]
    new_ref[...] = new
    scaled = (seen.reshape(slots, SPAN * WIN_R, LANES) * new[:, None, :]).reshape(pairs * PR, LANES)
    high = scaled.astype(jnp.bfloat16)
    low = (scaled - high.astype(jnp.float32)).astype(jnp.bfloat16)
    spread = jnp.dot(high, fold, preferred_element_type=jnp.float32)
    spread += jnp.dot(low, fold, preferred_element_type=jnp.float32)
    numer_ref[...] = jnp.where(keep, spread.reshape(pairs, PR, 2 * VOX), 0.0).sum(axis=1)


def update(picked, masked, traces, denom):
    slots = traces.shape[0]
    step = 8
    pairs = step * SPAN * 2
    trace_spec = pl.BlockSpec((step, LANES), lambda i: (i, 0))
    pair_spec = pl.BlockSpec((pairs, 2 * VOX), lambda i: (i, 0))
    return pl.pallas_call(
        update_kernel,
        grid=(slots // step,),
        in_specs=[pl.BlockSpec((pairs * PR, LANES), lambda i: (i, 0)), pair_spec, trace_spec, trace_spec],
        out_specs=[trace_spec, pair_spec],
        out_shape=[
            jax.ShapeDtypeStruct((slots, LANES), jnp.float32),
            jax.ShapeDtypeStruct((slots * SPAN * 2, 2 * VOX), jnp.float32),
        ],
        compiler_params=pltpu.CompilerParams(vmem_limit_bytes=32 * MIB),
        name="update_traces",
    )(picked, masked, traces, denom)


def finish_kernel(
    own_ref, own_ids_ref, cols_ref, col_ids_ref, traces_ref, other_traces_ref, col_traces_ref, other_col_ref,
    mine_ref, other_ref, out_ref, pair,
):
    @pl.when(pl.program_id(0) == 0)
    def _():
        def products(left, right):
            return lax.dot_general(
                left[...], right[...], (((1,), (1,)), ((), ())), precision=EXACT, preferred_element_type=jnp.float32
            )

        both = products(traces_ref, col_traces_ref) + products(other_traces_ref, other_col_ref)
        pair[...] = both * (1.0 / WIN_C)

    weight = jnp.where(own_ids_ref[0] == col_ids_ref[...], pair[...], 0.0)
    high = weight.astype(jnp.bfloat16)
    low = (weight - high.astype(jnp.float32)).astype(jnp.bfloat16)
    denom = jnp.dot(high, cols_ref[...], preferred_element_type=jnp.float32)
    denom += jnp.dot(low, cols_ref[...], preferred_element_type=jnp.float32)
    numer = mine_ref[...] + other_ref[...]
    out_ref[...] = (own_ref[...].astype(jnp.float32) * numer / (denom + EPSILON)).astype(jnp.bfloat16)


def finish(own, own_ids, cols, col_ids, traces, other_traces, col_traces, other_col, mine, other):
    slots = own.shape[0]
    width = cols.shape[0]
    block = pl.BlockSpec((slots, VOX), lambda b: (0, b))
    return pl.pallas_call(
        finish_kernel,
        grid=(NB,),
        in_specs=[
            block,
            pl.BlockSpec((1, slots, 1), lambda b: (b, 0, 0)),
            whole_spec(cols.shape),
            whole_spec(col_ids.shape),
            whole_spec(traces.shape),
            whole_spec(traces.shape),
            whole_spec(col_traces.shape),
            whole_spec(col_traces.shape),
            block,
            block,
        ],
        out_specs=block,
        out_shape=jax.ShapeDtypeStruct((slots, NB * VOX), jnp.bfloat16),
        scratch_shapes=[pltpu.VMEM((slots, width), jnp.float32)],
        compiler_params=pltpu.CompilerParams(vmem_limit_bytes=32 * MIB),
        name="new_footprints",
    )(own, own_ids, cols, col_ids, traces, other_traces, col_traces, other_col, mine, other)


def shards(movie, shifts, footprints, blocks, traces, counts):
    images, height, width = movie.shape[1:]
    tiles, me = lax.axis_size("tile"), lax.axis_index("tile")
    band = height // tiles
    pb = band // PR
    rb, xb = pb + 1, width // PC
    fh, slots = traces.shape[2], footprints.shape[0]
    frames = min(images, fh)
    planes = images // frames
    groups = fh // frames
    cap, step = 25, 5
    ups = [(i, i + 1) for i in range(tiles - 1)]
    downs = [(i + 1, i) for i in range(tiles - 1)]

    info = lax.all_gather(jnp.concatenate([blocks[:, 0], counts]), "tile")
    base, live_count = info[:, :slots], info[:, slots:]
    z, r, x = base // (rb * xb), (base // xb) % rb, base % xb
    live = jnp.arange(slots, dtype=jnp.int32) < live_count
    plane_ids = jnp.arange(Z, dtype=jnp.int32)
    cover = live[:, None, :] & (z[:, None, :] <= plane_ids[:, None]) & (plane_ids[:, None] < z[:, None, :] + SPAN)
    before = jnp.triu(jnp.ones((slots, slots), jnp.bfloat16), 1)
    rank = jnp.einsum(
        "tzk,kj->tzj", cover.astype(jnp.bfloat16), before, preferred_element_type=jnp.float32
    ).astype(jnp.int32)
    totals = cover.sum(axis=2, dtype=jnp.int32)
    rounds = (jnp.max(totals) + cap - 1) // cap

    first_plane = (me // groups) * planes
    my_place = lax.dynamic_slice_in_dim(jnp.where(cover, rank, -1), first_plane, planes, 1)
    my_totals = lax.dynamic_slice_in_dim(totals, first_plane, planes, 1)
    row_start = jnp.arange(tiles, dtype=jnp.int32)[:, None] * band + PR * r
    col_start = PC * x
    own_z = blocks[:, 0] // (rb * xb)
    own_live = jnp.arange(slots, dtype=jnp.int32) < counts[0]
    own_plane = own_z[:, None] + jnp.arange(SPAN, dtype=jnp.int32)
    own_place = lax.dynamic_index_in_dim(rank, me, 0, False)
    own_place = jnp.where(own_plane[:, :, None] == plane_ids, own_place.T[:, None, :], 0).sum(axis=2)
    source = (own_plane // planes) * groups

    def one_round(number, picked):
        offset = number * cap
        slot_ids = jnp.arange(cap, dtype=jnp.int32) + offset
        hit = my_place[:, :, None] == slot_ids[:, None]
        rows = jnp.where(hit, row_start[:, None, None, :], 0).sum(axis=3)
        cols = jnp.where(hit, col_start[:, None, None, :], 0).sum(axis=3)
        limits = jnp.clip(my_totals - offset, 0, cap)
        local = own_place - offset
        valid = own_live[:, None] & (local >= 0) & (local < cap)
        safe = jnp.clip(local, 0, cap - 1)
        received = []
        for d in range(planes):
            sent = extract(
                movie[0], shifts[0], rows[:, d], cols[:, d], limits[:, d], me % groups, cap, step, tiles, d, frames
            )
            received.append(lax.all_to_all(sent, "tile", split_axis=0, concat_axis=0, tiled=True))
        for d in range(planes):
            fresh = 0
            for g in range(groups):
                fresh = fresh + jnp.take(received[d], (source + g) * cap + safe, axis=0)
            old = jnp.zeros_like(fresh) if picked is None else picked
            picked = jnp.where((valid & (own_plane % planes == d))[:, :, None, None], fresh, old)
        return picked

    masked = jnp.where(own_live[:, None, None], footprints, jnp.zeros_like(footprints))
    halves = masked.reshape(slots, SPAN, 2, 2, VOX)
    by_block = lambda part: jnp.transpose(part, (1, 2, 0, 3)).reshape(-1, VOX)
    top = by_block(halves[:, :, 0])
    bottom = by_block(halves[:, :, 1])
    above = lax.ppermute(bottom, "tile", ups)
    below = lax.ppermute(top, "tile", downs)
    own_traces = traces[0]
    trace_above = lax.ppermute(own_traces, "tile", ups)
    trace_below = lax.ppermute(own_traces, "tile", downs)
    cols = jnp.concatenate([jnp.transpose(masked, (1, 0, 2)).reshape(-1, VOX), above, below], axis=0)

    def edge_ids(neighbour, d, row, shift):
        base_there = lax.dynamic_index_in_dim(base, jnp.clip(neighbour, 0, tiles - 1), 0, False)
        row_there = (base_there // xb) % rb + d
        steps = (jnp.arange(SPAN)[:, None] * rb * xb + d * xb + jnp.arange(2)).reshape(-1, 1).astype(jnp.int32)
        good = (row_there == row) & (neighbour >= 0) & (neighbour < tiles)
        return jnp.where(good, base_there + steps + shift, -1).reshape(-1)

    col_ids = jnp.concatenate(
        [blocks.T.reshape(-1), edge_ids(me - 1, 1, pb, -pb * xb), edge_ids(me + 1, 0, 0, pb * xb)]
    )[None]
    own_ids = blocks.T[:, :, None]
    own_flat = masked.reshape(slots, NB * VOX)

    def columns(own, up, down):
        return jnp.concatenate([jnp.tile(own, (NB, 1)), jnp.tile(up, (NB // 2, 1)), jnp.tile(down, (NB // 2, 1))])

    wide = lambda part: jnp.repeat(part, LANES // fh, axis=1)
    denom_c = overlaps(
        own_flat, own_ids, cols, col_ids, columns(wide(own_traces), wide(trace_above), wide(trace_below))
    )

    picked = one_round(0, None)
    _, picked = lax.while_loop(
        lambda state: state[0] < rounds,
        lambda state: (state[0] + 1, one_round(state[0], state[1])),
        (jnp.int32(1), picked),
    )
    new_wide, numer = update(
        picked.reshape(-1, LANES), masked.reshape(slots * SPAN * 2, 2 * VOX), wide(own_traces), denom_c
    )
    new = new_wide[:, :: LANES // fh]

    near, numer_other = exchange(new_wide, numer, tiles)
    new_footprints = finish(
        own_flat, own_ids, cols, col_ids, new_wide, near[0],
        columns(new_wide, near[1], near[3]), columns(near[0], near[2], near[4]),
        numer.reshape(slots, NB * VOX), numer_other.reshape(slots, NB * VOX),
    )
    return (new[None], new_footprints.reshape(slots, NB, VOX))


def solution(mesh):
    placed = (
        P("nrn", "tile", None, None),
        P("nrn", "tile", None),
        P("tile", None, None),
        P("tile", None),
        P("nrn", "tile", None),
        P("tile"),
    )
    return jax.shard_map(
        shards,
        mesh=mesh,
        in_specs=placed,
        out_specs=(P("nrn", "tile", None), P("tile", None, None)),
        check_vma=False,
    )
```

profile of v0, /device:TPU:9, one launch (start us, length us, event | category | flops | bytes accessed | tf_op | source)
XLA Modules:
  0.0 177.1 jit_solution(6477451978294967761)
XLA Ops:
  2.0 1.2 dynamic-slice
  4.1 10.1 %all-reduce = s32[1552]{0:T(1024)S(1)} all-reduce(s32[1552]{0:T(1024)S(1)} %add_dynamic-update-slice_fusion), channel_id=2, replica_groups=mesh['tile'=16,'nrn'=2] {'tile'}, use_global_device_ids=true, to_apply=%add | all-reduce | flops 1552 | bytes 12416
  15.3 1.8 select_reduce_fusion
  20.8 13.9 %extract_windows.16 = bf16[400,16,128]{2,1,0:T(8,128)(2,1)} custom-call(s32[400]{0:T(512)} %reshape_squeeze.16.rows_ref, s32[400]{0:T(512)} %reshape_squeeze.17.cols_ref, s32[16]{0:T(128)} %get-tuple-element.540.counts_ref, s32[16]{0:T(128)} %reshape_squeeze.18.shift_ref, s32[1]{0:T(128)} %constant.279.clone.1.group_ref, bf16[8,1024,1024]{2,1,0:T(8,128)(2,1)} %bitcast.112), custom_call_target="tpu_custom_call" | custom-call | tf_op jit(solution)/shard_map/extract_windows/pallas_call | solution.py:91
  34.7 4.7 %all-to-all-start.2 = ((bf16[400,16,128]{2,1,0:T(8,128)(2,1)}), bf16[400,16,128]{2,1,0:T(8,128)(2,1)S(1)}, u32[]{:S(2)}, u32[]{:S(2)}) async-start(bf16[400,16,128]{2,1,0:T(8,128)(2,1)} %extract_windows.16), calls=%async_computation.2 | async-start | bytes 3276800 | tf_op jit(solution)/shard_map/all_to_all | solution.py:381
  39.4 3.1 %collective-permute-start.2 = (f32[96,4]{0,1:T(4,128)S(1)}, f32[96,4]{0,1:T(4,128)S(1)}, u32[]{:S(2)}, u32[]{:S(2)}) collective-permute-start(f32[96,4]{0,1:T(4,128)S(1)} %bitcast.140), channel_id=1, source_target_pairs={{0,2},{2,4},{4,6},{6,8},{8,10},{10,12},{12,14},{14,16},{16,18},{18... | collective-permute-start | bytes 4616 | tf_op jit(solution)/shard_map/ppermute | solution.py:398
  42.5 4.0 %collective-permute-start.3 = (f32[96,4]{0,1:T(4,128)S(1)}, f32[96,4]{0,1:T(4,128)S(1)}, u32[]{:S(2)}, u32[]{:S(2)}) collective-permute-start(f32[96,4]{0,1:T(4,128)S(1)} %bitcast.141), channel_id=1, source_target_pairs={{2,0},{4,2},{6,4},{8,6},{10,8},{12,10},{14,12},{16,14},{18,16},{20... | collective-permute-start | bytes 4616 | tf_op jit(solution)/shard_map/ppermute | solution.py:399
  47.7 1.9 %collective-permute-start = (bf16[768,128]{1,0:T(8,128)(2,1)}, bf16[768,128]{1,0:T(8,128)(2,1)}, u32[]{:S(2)}, u32[]{:S(2)}) collective-permute-start(bf16[768,128]{1,0:T(8,128)(2,1)} %bitcast.20), channel_id=1, source_target_pairs={{0,2},{2,4},{4,6},{6,8},{8,10},{10,12},{12,14},{14,16},{16,18},{18... | collective-permute-start | bytes 589832 | tf_op jit(solution)/shard_map/ppermute | solution.py:395
  50.4 5.1 %collective-permute-start.1 = (bf16[768,128]{1,0:T(8,128)(2,1)}, bf16[768,128]{1,0:T(8,128)(2,1)}, u32[]{:S(2)}, u32[]{:S(2)}) collective-permute-start(bf16[768,128]{1,0:T(8,128)(2,1)} %bitcast.23), channel_id=1, source_target_pairs={{2,0},{4,2},{6,4},{8,6},{10,8},{12,10},{14,12},{16,14},{18,16},{20... | collective-permute-start | bytes 589832 | tf_op jit(solution)/shard_map/ppermute | solution.py:396
  57.0 14.3 %extract_windows.17 = bf16[400,16,128]{2,1,0:T(8,128)(2,1)} custom-call(s32[400]{0:T(512)} %reshape_squeeze.19.rows_ref, s32[400]{0:T(512)} %reshape_squeeze.20.cols_ref, s32[16]{0:T(128)} %get-tuple-element.541.counts_ref, s32[16]{0:T(128)} %reshape_squeeze.18.shift_ref, s32[1]{0:T(128)} %constant.279.clone.1.group_ref, bf16[8,1024,1024]{2,1,0:T(8,128)(2,1)} %bitcast.113), custom_call_target="tpu_custom_call" | custom-call | tf_op jit(solution)/shard_map/extract_windows/pallas_call | solution.py:91
  71.4 4.5 %all-to-all-done.2 = bf16[400,16,128]{2,1,0:T(8,128)(2,1)S(1)} async-done(((bf16[400,16,128]{2,1,0:T(8,128)(2,1)}), bf16[400,16,128]{2,1,0:T(8,128)(2,1)S(1)}, u32[]{:S(2)}, u32[]{:S(2)}) %all-to-all-start.2) | async-done | bytes 1638432 | tf_op jit(solution)/shard_map/all_to_all | solution.py:381
  75.9 1.2 copy-done.4
  77.1 5.9 %all-to-all-start.3 = ((bf16[400,16,128]{2,1,0:T(8,128)(2,1)}), bf16[400,16,128]{2,1,0:T(8,128)(2,1)}, u32[]{:S(2)}, u32[]{:S(2)}) async-start(bf16[400,16,128]{2,1,0:T(8,128)(2,1)} %extract_windows.17), calls=%async_computation.3 | async-start | bytes 3276800 | tf_op jit(solution)/shard_map/all_to_all | solution.py:381
  86.2 0.8 copy.135
  88.1 0.9 copy-done.5
  88.9 1.1 pad_maximum_fusion.3.cols_ref
  90.0 9.4 %denom_c.1.denom_ref = f32[96,128]{1,0:T(8,128)S(1)} custom-call(bf16[96,2048]{1,0:T(8,128)(2,1)S(1)} %bitcast.107, s32[16,96,1]{2,1,0:T(8,128)S(1)} %copy.141.own_ids_ref, bf16[3072,128]{1,0:T(8,128)(2,1)S(1)} %pad_maximum_fusion.3.cols_ref, s32[1,3072]{1,0:T(1,128)S(1)} %bitcast.110, f32[3072,128]{1,0:T(8,128)S(1)} %pad_maximum_fusion.traces_ref), custom_call_target="tpu_custom_call" | custom-call | tf_op jit(solution)/shard_map/denom_c/pallas_call | solution.py:210
  99.4 3.5 %gather_fusion.2 = bf16[384,16,128]{2,1,0:T(8,128)(2,1)} fusion(bf16[400,16,128]{2,1,0:T(8,128)(2,1)} %copy-done.4, s32[1024]{0:T(1024)S(1)} %pad_clamp_fusion.1), kind=kCustom, calls=%fused_computation.clone | custom fusion | bytes 3147264 | tf_op jit(solution)/shard_map/jit(_take)/gather | solution.py:385
  102.9 17.4 %all-to-all-done.3 = bf16[400,16,128]{2,1,0:T(8,128)(2,1)} async-done(((bf16[400,16,128]{2,1,0:T(8,128)(2,1)}), bf16[400,16,128]{2,1,0:T(8,128)(2,1)}, u32[]{:S(2)}, u32[]{:S(2)}) %all-to-all-start.3) | async-done | bytes 1638432 | tf_op jit(solution)/shard_map/all_to_all | solution.py:381
  120.3 3.5 %gather_fusion.3 = bf16[384,16,128]{2,1,0:T(8,128)(2,1)} fusion(bf16[400,16,128]{2,1,0:T(8,128)(2,1)} %all-to-all-done.3, s32[1024]{0:T(1024)S(1)} %pad_clamp_fusion.1), kind=kCustom, calls=%fused_computation.2.clone | custom fusion | bytes 3147264 | tf_op jit(solution)/shard_map/jit(_take)/gather | solution.py:385
  123.8 5.5 %fusion.17 = bf16[96,4,16,128]{3,2,1,0:T(8,128)(2,1)} fusion(bf16[96,4,16,128]{3,2,1,0:T(8,128)(2,1)} %bitcast.122, bf16[96,4,16,128]{3,2,1,0:T(8,128)(2,1)} %bitcast.121, pred[96,4]{1,0:T(8,128)(4,1)S(1)} %copy.121, pred[96,4]{1,0:T(8,128)(4,1)S(1)} %copy.127, pred[96,4]{1,0:T(8,128)(4,1)S(1)} %copy.120), kind=kLoop, calls=%fused_computation.42 | loop fusion | flops 3145728 | bytes 4719744 | tf_op jit(solution)/shard_map/jit(_where)/select_n | solution.py:387
  129.3 11.3 %update_traces.1 = (f32[96,128]{1,0:T(8,128)S(1)}, f32[768,256]{1,0:T(8,128)S(1)}) custom-call(bf16[6144,128]{1,0:T(8,128)(2,1)} %bitcast.118, bf16[768,256]{1,0:T(8,128)(2,1)S(1)} %reshape.362.masked_ref, f32[96,128]{1,0:T(8,128)S(1)} %copy.142.traces_ref, f32[96,128]{1,0:T(8,128)S(1)} %denom_c.1.denom_ref), custom_call_target="tpu_custom_call" | custom-call | tf_op jit(solution)/shard_map/update_traces/pallas_call | solution.py:263
  142.2 10.6 %exchange.1 = (f32[5,96,128]{2,1,0:T(8,128)}, f32[768,256]{1,0:T(8,128)}) custom-call(f32[96,128]{1,0:T(8,128)} %copy-done.1, f32[768,256]{1,0:T(8,128)} %copy-done), custom_call_target="tpu_custom_call" | custom-call | tf_op jit(solution)/shard_map/exchange/pallas_call | solution.py:167
  152.8 1.5 slice.118
  154.3 1.6 slice_bitcast_fusion.3
  155.9 1.3 reshape.371.other_ref
  157.2 0.9 tile.101
  158.1 0.8 tile.104
  158.9 0.8 tile.107
  161.5 13.4 %new_footprints.1 = bf16[96,2048]{1,0:T(8,128)(2,1)S(1)} custom-call(bf16[96,2048]{1,0:T(8,128)(2,1)S(1)} %bitcast.108, s32[16,96,1]{2,1,0:T(8,128)S(1)} %copy.141.own_ids_ref, bf16[3072,128]{1,0:T(8,128)(2,1)S(1)} %pad_maximum_fusion.3.cols_ref, s32[1,3072]{1,0:T(1,128)S(1)} %bitcast.111, f32[96,128]{1,0:T(8,128)S(1)} %copy-done.2, ...), custom_call_target="tpu_custom_call" | custom-call | tf_op jit(solution)/shard_map/new_footprints/pallas_call | solution.py:304
  174.8 0.8 copy.148
  175.7 1.4 copy.144
  (104 shorter events, 15.7 us)
Async XLA Ops:
  20.2 65.3 %copy-start.9 = (s32[1,8,2]{2,1,0:T(8,128)}, s32[1,8,2]{2,1,0:T(8,128)S(1)}, u32[]{:S(2)}) copy-start(s32[1,8,2]{2,1,0:T(8,128)S(1)} %copy.125) | copy-start | bytes 196
  34.7 4.7 %copy-start.11 = (f32[1,96,4]{1,2,0:T(4,128)S(1)}, f32[1,96,4]{1,2,0:T(4,128)}, u32[]{:S(2)}) copy-start(f32[1,96,4]{1,2,0:T(4,128)} %param.16) | copy-start | bytes 4612
  34.7 11.8 %copy-start.6 = (bf16[96,16,128]{2,1,0:T(8,128)(2,1)S(1)}, bf16[96,16,128]{2,1,0:T(8,128)(2,1)}, u32[]{:S(2)}) copy-start(bf16[96,16,128]{2,1,0:T(8,128)(2,1)} %param.14) | copy-start | bytes 1179652
  34.7 41.2 %all-to-all-start.2 = ((bf16[400,16,128]{2,1,0:T(8,128)(2,1)}), bf16[400,16,128]{2,1,0:T(8,128)(2,1)S(1)}, u32[]{:S(2)}, u32[]{:S(2)}) async-start(bf16[400,16,128]{2,1,0:T(8,128)(2,1)} %extract_windows.16), calls=%async_computation.2 | async-start | bytes 3276800 | tf_op jit(solution)/shard_map/all_to_all | solution.py:381
  39.4 48.1 %collective-permute-start.2 = (f32[96,4]{0,1:T(4,128)S(1)}, f32[96,4]{0,1:T(4,128)S(1)}, u32[]{:S(2)}, u32[]{:S(2)}) collective-permute-start(f32[96,4]{0,1:T(4,128)S(1)} %bitcast.140), channel_id=1, source_target_pairs={{0,2},{2,4},{4,6},{6,8},{8,10},{10,12},{12,14},{14,16},{16,18},{18... | collective-permute-start | bytes 4616 | tf_op jit(solution)/shard_map/ppermute | solution.py:398
  42.5 45.1 %collective-permute-start.3 = (f32[96,4]{0,1:T(4,128)S(1)}, f32[96,4]{0,1:T(4,128)S(1)}, u32[]{:S(2)}, u32[]{:S(2)}) collective-permute-start(f32[96,4]{0,1:T(4,128)S(1)} %bitcast.141), channel_id=1, source_target_pairs={{2,0},{4,2},{6,4},{8,6},{10,8},{12,10},{14,12},{16,14},{18,16},{20... | collective-permute-start | bytes 4616 | tf_op jit(solution)/shard_map/ppermute | solution.py:399
  47.7 40.3 %collective-permute-start = (bf16[768,128]{1,0:T(8,128)(2,1)}, bf16[768,128]{1,0:T(8,128)(2,1)}, u32[]{:S(2)}, u32[]{:S(2)}) collective-permute-start(bf16[768,128]{1,0:T(8,128)(2,1)} %bitcast.20), channel_id=1, source_target_pairs={{0,2},{2,4},{4,6},{6,8},{8,10},{10,12},{12,14},{14,16},{16,18},{18... | collective-permute-start | bytes 589832 | tf_op jit(solution)/shard_map/ppermute | solution.py:395
  50.4 37.7 %collective-permute-start.1 = (bf16[768,128]{1,0:T(8,128)(2,1)}, bf16[768,128]{1,0:T(8,128)(2,1)}, u32[]{:S(2)}, u32[]{:S(2)}) collective-permute-start(bf16[768,128]{1,0:T(8,128)(2,1)} %bitcast.23), channel_id=1, source_target_pairs={{2,0},{4,2},{6,4},{8,6},{10,8},{12,10},{14,12},{16,14},{18,16},{20... | collective-permute-start | bytes 589832 | tf_op jit(solution)/shard_map/ppermute | solution.py:396
  71.4 12.5 %copy-start.10 = (s32[96,16]{0,1:T(8,128)S(1)}, s32[96,16]{0,1:T(8,128)}, u32[]{:S(2)}) copy-start(s32[96,16]{0,1:T(8,128)} %param.15) | copy-start | bytes 18436
  75.9 1.2 copy-start.4
  77.1 43.2 %all-to-all-start.3 = ((bf16[400,16,128]{2,1,0:T(8,128)(2,1)}), bf16[400,16,128]{2,1,0:T(8,128)(2,1)}, u32[]{:S(2)}, u32[]{:S(2)}) async-start(bf16[400,16,128]{2,1,0:T(8,128)(2,1)} %extract_windows.17), calls=%async_computation.3 | async-start | bytes 3276800 | tf_op jit(solution)/shard_map/all_to_all | solution.py:381
  87.9 1.0 copy-start.5
  140.6 0.6 copy-start.1
  141.3 0.9 copy-start
  159.7 0.8 copy-start.8
  159.7 0.8 copy-start.7
  159.7 0.9 copy-start.2
  160.7 0.8 copy-start.3
where the time goes:
time: 178 us; the launch traced here: 177 us
  Pallas kernels  72.9 us (41%)
  local copies, waits for them, and re-layouts  32.5 us (18%)
  starting transfers between devices  24.8 us (14%)
  waiting for transfers between devices  21.9 us (12%)
  other arithmetic  11.5 us (6%)
  blocking collectives  10.1 us (6%)
  between operations  3.15 us (2%)
    pallas_call x2, Pallas kernels, extract(): pl.pallas_call(functools.partial(extract_kernel, cap, step, tiles, plane,...  28.2 us
    all_to_all x2, waiting for transfers between devices, one_round(): lax.all_to_all(sent, 'tile', split_axis=0, concat_axis=0, tiled=True)  21.9 us
    pallas_call x1, Pallas kernels, finish(): pl.pallas_call(finish_kernel, grid=(NB,), in_specs=[block, pl.BlockSpec((...  13.4 us
    pallas_call x1, Pallas kernels, update(): pl.pallas_call(update_kernel, grid=(slots // step,), in_specs=[pl.BlockSp...  11.3 us
    unnamed x33, local copies, waits for them, and re-layouts  10.7 us
    pallas_call x1, Pallas kernels, exchange(): pl.pallas_call(functools.partial(exchange_kernel, tiles), in_specs=[anywh...  10.6 us
    all_to_all x2, starting transfers between devices, one_round(): lax.all_to_all(sent, 'tile', split_axis=0, concat_axis=0, tiled=True)  10.6 us
    unnamed x1, blocking collectives  10.1 us
  transfers between devices with their start and end apart: 6, of which 2 were waited for; matrix products, arithmetic and copies ran while one was open for 7% of the time, Pallas kernels for 13%

commit v1 on v0

--- a/solution.py
+++ b/solution.py
@@ -225,24 +225,66 @@
     )(own, own_ids, cols, col_ids, col_traces)
 
 
-def update_kernel(picked_ref, masked_ref, traces_ref, denom_ref, new_ref, numer_ref):
-    pairs = masked_ref.shape[0]
-    slots = traces_ref.shape[0]
-    keep_lane = lax.broadcasted_iota(jnp.int32, (pairs, PR, 2 * VOX), 2)
-    keep_row = lax.broadcasted_iota(jnp.int32, (pairs, PR, 2 * VOX), 1)
-    keep = (keep_lane & (VOX - 1)) // PC == keep_row
+def row_keeper(pairs):
+    lane = lax.broadcasted_iota(jnp.int32, (pairs, PR, 2 * VOX), 2)
+    row = lax.broadcasted_iota(jnp.int32, (pairs, PR, 2 * VOX), 1)
+    return (lane & (VOX - 1)) // PC == row
+
+
+def fold_matrix():
     out_lane = lax.broadcasted_iota(jnp.int32, (LANES, 2 * VOX), 1)
     in_lane = lax.broadcasted_iota(jnp.int32, (LANES, 2 * VOX), 0)
-    fold = ((in_lane & (WIN_C - 1)) == (out_lane // VOX) * PC + (out_lane & (PC - 1))).astype(jnp.bfloat16)
+    return ((in_lane & (WIN_C - 1)) == (out_lane // VOX) * PC + (out_lane & (PC - 1))).astype(jnp.bfloat16)
+
+
+def feet_kernel(masked_ref, out_ref):
+    pairs = masked_ref.shape[0]
+    feet = masked_ref[...].astype(jnp.float32)
+    feet = jnp.where(row_keeper(pairs), feet[:, None, :], 0.0).reshape(pairs * PR, 2 * VOX).astype(jnp.bfloat16)
+    feet = lax.dot_general(feet, fold_matrix(), (((1,), (1,)), ((), ())), preferred_element_type=jnp.float32)
+    out_ref[...] = feet.astype(jnp.bfloat16)
+
+
+def window_feet(masked):
+    total = masked.shape[0]
+    pairs = total // 4
+    return pl.pallas_call(
+        feet_kernel,
+        grid=(4,),
+        in_specs=[pl.BlockSpec((pairs, 2 * VOX), lambda i: (i, 0))],
+        out_specs=pl.BlockSpec((pairs * PR, LANES), lambda i: (i, 0)),
+        out_shape=jax.ShapeDtypeStruct((total * PR, LANES), jnp.bfloat16),
+        compiler_params=pltpu.CompilerParams(vmem_limit_bytes=32 * MIB),
+        name="window_feet",
+    )(masked)
+
+
+def update_kernel(
+    cap, groups, planes, index_ref, feet_ref, extra_ref, traces_ref, denom_ref, *refs
+):
+    received, (new_ref, numer_ref, windows) = refs[:planes], refs[planes:]
+    slots = traces_ref.shape[0]
+    count = slots * SPAN
+    pairs = count * 2
+    length = received[0].shape[0]
+    first = pl.program_id(0) * count
+    for w in range(count):
+        index = index_ref[first + w]
+        window = extra_ref[w].astype(jnp.float32)
+        for d in range(planes):
+            at = jnp.clip(index - d * length, 0, length - 1 - (groups - 1) * cap)
+            got = received[d][at].astype(jnp.float32)
+            for g in range(1, groups):
+                got += received[d][at + g * cap].astype(jnp.float32)
+            window = jnp.where(index >= d * length, got, window)
+        windows[pl.ds(w * WIN_R, WIN_R), :] = window
+
     group_a = lax.broadcasted_iota(jnp.int32, (LANES, LANES), 0) // WIN_C
     group_b = lax.broadcasted_iota(jnp.int32, (LANES, LANES), 1) // WIN_C
     group_sum = (group_a == group_b).astype(jnp.float32)
-
-    feet = masked_ref[...].astype(jnp.float32)
-    feet = jnp.where(keep, feet[:, None, :], 0.0).reshape(pairs * PR, 2 * VOX).astype(jnp.bfloat16)
-    feet = lax.dot_general(feet, fold, (((1,), (1,)), ((), ())), preferred_element_type=jnp.float32)
-    seen = picked_ref[...].astype(jnp.float32)
-    sums = (feet * seen).reshape(slots, SPAN * WIN_R, LANES).sum(axis=1)
+    fold = fold_matrix()
+    seen = windows[...]
+    sums = (feet_ref[...].astype(jnp.float32) * seen).reshape(slots, SPAN * WIN_R, LANES).sum(axis=1)
     numer_c = jnp.dot(sums, group_sum, precision=EXACT, preferred_element_type=jnp.float32)
     new = traces_ref[...] * numer_c / denom_ref[...]
     new_ref[...] = new
@@ -251,77 +293,86 @@
     low = (scaled - high.astype(jnp.float32)).astype(jnp.bfloat16)
     spread = jnp.dot(high, fold, preferred_element_type=jnp.float32)
     spread += jnp.dot(low, fold, preferred_element_type=jnp.float32)
-    numer_ref[...] = jnp.where(keep, spread.reshape(pairs, PR, 2 * VOX), 0.0).sum(axis=1)
-
-
-def update(picked, masked, traces, denom):
+    numer = jnp.where(row_keeper(pairs), spread.reshape(pairs, PR, 2 * VOX), 0.0).sum(axis=1)
+    for e in range(2):
+        numer_ref[e] = numer[:, e * VOX : (e + 1) * VOX]
+
+
+def update(index, feet, extra, traces, denom, received, cap, groups):
     slots = traces.shape[0]
-    step = 8
+    step = 24
     pairs = step * SPAN * 2
     trace_spec = pl.BlockSpec((step, LANES), lambda i: (i, 0))
-    pair_spec = pl.BlockSpec((pairs, 2 * VOX), lambda i: (i, 0))
+    numer_spec = pl.BlockSpec((2, pairs, VOX), lambda i: (0, i, 0))
     return pl.pallas_call(
-        update_kernel,
+        functools.partial(update_kernel, cap, groups, len(received)),
         grid=(slots // step,),
-        in_specs=[pl.BlockSpec((pairs * PR, LANES), lambda i: (i, 0)), pair_spec, trace_spec, trace_spec],
-        out_specs=[trace_spec, pair_spec],
+        in_specs=[
+            pl.BlockSpec(memory_space=pltpu.SMEM),
+            pl.BlockSpec((pairs * PR, LANES), lambda i: (i, 0)),
+            pl.BlockSpec((step * SPAN, WIN_R, LANES), lambda i: (i, 0, 0)),
+            trace_spec,
+            trace_spec,
+        ]
+        + [whole_spec(part.shape) for part in received],
+        out_specs=[trace_spec, numer_spec],
         out_shape=[
             jax.ShapeDtypeStruct((slots, LANES), jnp.float32),
-            jax.ShapeDtypeStruct((slots * SPAN * 2, 2 * VOX), jnp.float32),
+            jax.ShapeDtypeStruct((2, slots * SPAN * 2, VOX), jnp.float32),
         ],
-        compiler_params=pltpu.CompilerParams(vmem_limit_bytes=32 * MIB),
+        scratch_shapes=[pltpu.VMEM((pairs * PR, LANES), jnp.float32)],
+        compiler_params=pltpu.CompilerParams(vmem_limit_bytes=48 * MIB),
         name="update_traces",
-    )(picked, masked, traces, denom)
+    )(index, feet, extra, traces, denom, *received)
 
 
 def finish_kernel(
-    own_ref, own_ids_ref, cols_ref, col_ids_ref, traces_ref, other_traces_ref, col_traces_ref, other_col_ref,
-    mine_ref, other_ref, out_ref, pair,
+    own_ref, own_ids_ref, cols_ref, col_ids_ref, new_ref, near_ref, mine_ref, other_ref, out_ref, pair
 ):
-    @pl.when(pl.program_id(0) == 0)
-    def _():
-        def products(left, right):
+    j = pl.program_id(0)
+    slots = new_ref.shape[0]
+
+    @pl.when(j == 0)
+    def _():
+        def products(own, up, down):
+            columns = jnp.concatenate([own] * NB + [up] * (NB // 2) + [down] * (NB // 2), axis=0)
             return lax.dot_general(
-                left[...], right[...], (((1,), (1,)), ((), ())), precision=EXACT, preferred_element_type=jnp.float32
+                own, columns, (((1,), (1,)), ((), ())), precision=EXACT, preferred_element_type=jnp.float32
             )
 
-        both = products(traces_ref, col_traces_ref) + products(other_traces_ref, other_col_ref)
+        both = products(new_ref[...], near_ref[1], near_ref[3])
+        both += products(near_ref[0], near_ref[2], near_ref[4])
         pair[...] = both * (1.0 / WIN_C)
 
-    weight = jnp.where(own_ids_ref[0] == col_ids_ref[...], pair[...], 0.0)
-    high = weight.astype(jnp.bfloat16)
-    low = (weight - high.astype(jnp.float32)).astype(jnp.bfloat16)
-    denom = jnp.dot(high, cols_ref[...], preferred_element_type=jnp.float32)
-    denom += jnp.dot(low, cols_ref[...], preferred_element_type=jnp.float32)
-    numer = mine_ref[...] + other_ref[...]
-    out_ref[...] = (own_ref[...].astype(jnp.float32) * numer / (denom + EPSILON)).astype(jnp.bfloat16)
-
-
-def finish(own, own_ids, cols, col_ids, traces, other_traces, col_traces, other_col, mine, other):
+    highs, lows = [], []
+    for e in range(2):
+        weight = jnp.where(own_ids_ref[e] == col_ids_ref[...], pair[...], 0.0)
+        highs.append(weight.astype(jnp.bfloat16))
+        lows.append((weight - highs[-1].astype(jnp.float32)).astype(jnp.bfloat16))
+    sums = jnp.dot(jnp.concatenate(highs + lows, axis=0), cols_ref[...], preferred_element_type=jnp.float32)
+    for e in range(2):
+        denom = sums[e * slots : (e + 1) * slots] + sums[(e + 2) * slots : (e + 3) * slots]
+        at = pl.ds(e * slots * (NB // 2) + j, slots, stride=NB // 2)
+        numer = mine_ref[at, :] + other_ref[at, :]
+        lanes = pl.ds(e * VOX, VOX)
+        out_ref[:, lanes] = (own_ref[:, lanes].astype(jnp.float32) * numer / (denom + EPSILON)).astype(jnp.bfloat16)
+
+
+def finish(own, own_ids, cols, col_ids, new, near, mine, other):
     slots = own.shape[0]
     width = cols.shape[0]
-    block = pl.BlockSpec((slots, VOX), lambda b: (0, b))
+    block = pl.BlockSpec((slots, 2 * VOX), lambda j: (0, j))
     return pl.pallas_call(
         finish_kernel,
-        grid=(NB,),
-        in_specs=[
-            block,
-            pl.BlockSpec((1, slots, 1), lambda b: (b, 0, 0)),
-            whole_spec(cols.shape),
-            whole_spec(col_ids.shape),
-            whole_spec(traces.shape),
-            whole_spec(traces.shape),
-            whole_spec(col_traces.shape),
-            whole_spec(col_traces.shape),
-            block,
-            block,
-        ],
+        grid=(NB // 2,),
+        in_specs=[block, pl.BlockSpec((2, slots, 1), lambda j: (j, 0, 0))]
+        + [whole_spec(part.shape) for part in (cols, col_ids, new, near, mine, other)],
         out_specs=block,
         out_shape=jax.ShapeDtypeStruct((slots, NB * VOX), jnp.bfloat16),
         scratch_shapes=[pltpu.VMEM((slots, width), jnp.float32)],
-        compiler_params=pltpu.CompilerParams(vmem_limit_bytes=32 * MIB),
+        compiler_params=pltpu.CompilerParams(vmem_limit_bytes=48 * MIB),
         name="new_footprints",
-    )(own, own_ids, cols, col_ids, traces, other_traces, col_traces, other_col, mine, other)
+    )(own, own_ids, cols, col_ids, new, near, mine, other)
 
 
 def shards(movie, shifts, footprints, blocks, traces, counts):
@@ -338,8 +389,11 @@
     ups = [(i, i + 1) for i in range(tiles - 1)]
     downs = [(i + 1, i) for i in range(tiles - 1)]
 
-    info = lax.all_gather(jnp.concatenate([blocks[:, 0], counts]), "tile")
-    base, live_count = info[:, :slots], info[:, slots:]
+    own_traces = traces[0]
+    numbers = jnp.concatenate([blocks[:, 0], counts]).astype(jnp.float32)
+    info = lax.all_gather(jnp.concatenate([numbers, own_traces.reshape(-1)]), "tile")
+    base, live_count = info[:, :slots].astype(jnp.int32), info[:, slots : slots + 1].astype(jnp.int32)
+    all_traces = info[:, slots + 1 :].reshape(tiles, slots, fh)
     z, r, x = base // (rb * xb), (base // xb) % rb, base % xb
     live = jnp.arange(slots, dtype=jnp.int32) < live_count
     plane_ids = jnp.arange(Z, dtype=jnp.int32)
@@ -363,29 +417,33 @@
     own_place = jnp.where(own_plane[:, :, None] == plane_ids, own_place.T[:, None, :], 0).sum(axis=2)
     source = (own_plane // planes) * groups
 
-    def one_round(number, picked):
+    def one_round(number):
         offset = number * cap
         slot_ids = jnp.arange(cap, dtype=jnp.int32) + offset
         hit = my_place[:, :, None] == slot_ids[:, None]
         rows = jnp.where(hit, row_start[:, None, None, :], 0).sum(axis=3)
         cols = jnp.where(hit, col_start[:, None, None, :], 0).sum(axis=3)
         limits = jnp.clip(my_totals - offset, 0, cap)
-        local = own_place - offset
-        valid = own_live[:, None] & (local >= 0) & (local < cap)
-        safe = jnp.clip(local, 0, cap - 1)
         received = []
         for d in range(planes):
             sent = extract(
                 movie[0], shifts[0], rows[:, d], cols[:, d], limits[:, d], me % groups, cap, step, tiles, d, frames
             )
             received.append(lax.all_to_all(sent, "tile", split_axis=0, concat_axis=0, tiled=True))
+        local = own_place - offset
+        valid = own_live[:, None] & (local >= 0) & (local < cap)
+        index = source * cap + jnp.clip(local, 0, cap - 1)
+        return received, index, valid
+
+    def later_round(state):
+        number, picked = state
+        received, index, valid = one_round(number)
         for d in range(planes):
             fresh = 0
             for g in range(groups):
-                fresh = fresh + jnp.take(received[d], (source + g) * cap + safe, axis=0)
-            old = jnp.zeros_like(fresh) if picked is None else picked
-            picked = jnp.where((valid & (own_plane % planes == d))[:, :, None, None], fresh, old)
-        return picked
+                fresh = fresh + jnp.take(received[d], index + g * cap, axis=0)
+            picked = jnp.where((valid & (own_plane % planes == d))[:, :, None, None], fresh, picked)
+        return number + 1, picked
 
     masked = jnp.where(own_live[:, None, None], footprints, jnp.zeros_like(footprints))
     halves = masked.reshape(slots, SPAN, 2, 2, VOX)
@@ -394,9 +452,8 @@
     bottom = by_block(halves[:, :, 1])
     above = lax.ppermute(bottom, "tile", ups)
     below = lax.ppermute(top, "tile", downs)
-    own_traces = traces[0]
-    trace_above = lax.ppermute(own_traces, "tile", ups)
-    trace_below = lax.ppermute(own_traces, "tile", downs)
+    trace_above = lax.dynamic_index_in_dim(all_traces, jnp.maximum(me - 1, 0), 0, False)
+    trace_below = lax.dynamic_index_in_dim(all_traces, jnp.minimum(me + 1, tiles - 1), 0, False)
     cols = jnp.concatenate([jnp.transpose(masked, (1, 0, 2)).reshape(-1, VOX), above, below], axis=0)
 
     def edge_ids(neighbour, d, row, shift):
@@ -420,23 +477,23 @@
         own_flat, own_ids, cols, col_ids, columns(wide(own_traces), wide(trace_above), wide(trace_below))
     )
 
-    picked = one_round(0, None)
-    _, picked = lax.while_loop(
+    pair_feet = masked.reshape(slots * SPAN * 2, 2 * VOX)
+    feet = window_feet(pair_feet)
+    received, index, valid = one_round(0)
+    index = jnp.where(valid, index + (own_plane % planes) * (tiles * cap), -1).reshape(-1)
+    _, later = lax.while_loop(
         lambda state: state[0] < rounds,
-        lambda state: (state[0] + 1, one_round(state[0], state[1])),
-        (jnp.int32(1), picked),
+        later_round,
+        (jnp.int32(1), jnp.zeros((slots, SPAN, WIN_R, LANES), jnp.bfloat16)),
     )
     new_wide, numer = update(
-        picked.reshape(-1, LANES), masked.reshape(slots * SPAN * 2, 2 * VOX), wide(own_traces), denom_c
+        index, feet, later.reshape(-1, WIN_R, LANES), wide(own_traces), denom_c, received, cap, groups
     )
     new = new_wide[:, :: LANES // fh]
 
+    numer = numer.reshape(-1, VOX)
     near, numer_other = exchange(new_wide, numer, tiles)
-    new_footprints = finish(
-        own_flat, own_ids, cols, col_ids, new_wide, near[0],
-        columns(new_wide, near[1], near[3]), columns(near[0], near[2], near[4]),
-        numer.reshape(slots, NB * VOX), numer_other.reshape(slots, NB * VOX),
-    )
+    new_footprints = finish(own_flat, own_ids, cols, col_ids, new_wide, near, numer, numer_other)
     return (new[None], new_footprints.reshape(slots, NB, VOX))
 
 

time: 178 us -> 206 us (1.16)
  blocking collectives: 10.1 us -> 56.8 us
  local copies, waits for them, and re-layouts: 32.5 us -> 25.9 us
  starting transfers between devices: 24.8 us -> 19.3 us
  other arithmetic: 11.5 us -> 6.14 us
    unnamed x1, blocking collectives: 10.1 us -> 56.8 us
    ppermute x2 -> x0, starting transfers between devices: 7.08 us -> none  [the longest x1 3.99 us: shards(): trace_below = lax.ppermute(own_traces, 'tile', downs)]
    gather x2 -> x0, local copies, waits for them, and re-layouts: 7.02 us -> none  [one_round(): fresh = fresh + jnp.take(received[d], (source + g) * cap + safe, axis=0)]
    select_n x1, other arithmetic: 5.51 us -> 0.01 us  [shards(): jnp.where(valid, index + own_plane % planes * (tiles * cap), -1).reshape(-1)]
    unnamed x33 -> x43, local copies, waits for them, and re-layouts: 10.7 us -> 15.9 us
    pallas_call x2 -> x3, Pallas kernels: 24.7 us -> 19.9 us  [the longest x1 10.4 us: finish(): pl.pallas_call(finish_kernel, grid=(NB // 2,), in_specs=[block, pl.BlockS...]
    all_to_all x2, starting transfers between devices: 10.6 us -> 13.4 us  [one_round(): lax.all_to_all(sent, 'tile', split_axis=0, concat_axis=0, tiled=True)]
    pallas_call x1, Pallas kernels: 10.6 us -> 13.1 us  [exchange(): pl.pallas_call(functools.partial(exchange_kernel, tiles), in_specs=[anywh...]
  transfers between devices with their start and end apart: 6 -> 4, of which waited for: 2 -> 2; matrix products, arithmetic and copies ran while one was open for 7% -> 4% of each run, Pallas kernels for 13% -> 13%
where the time goes in v1:
time: 206 us
  Pallas kernels  71.9 us (35%)
  blocking collectives  56.8 us (28%)
  local copies, waits for them, and re-layouts  25.9 us (13%)
  waiting for transfers between devices  22.6 us (11%)
  starting transfers between devices  19.3 us (9%)
  other arithmetic  6.14 us (3%)
  between operations  3.05 us (1%)
    unnamed x1, blocking collectives  56.8 us
    pallas_call x2, Pallas kernels, extract(): pl.pallas_call(functools.partial(extract_kernel, cap, step, tiles, plane,...  29.4 us
    all_to_all x2, waiting for transfers between devices, one_round(): lax.all_to_all(sent, 'tile', split_axis=0, concat_axis=0, tiled=True)  22.6 us
    unnamed x43, local copies, waits for them, and re-layouts  15.9 us
    all_to_all x2, starting transfers between devices, one_round(): lax.all_to_all(sent, 'tile', split_axis=0, concat_axis=0, tiled=True)  13.4 us
    pallas_call x1, Pallas kernels, exchange(): pl.pallas_call(functools.partial(exchange_kernel, tiles), in_specs=[anywh...  13.1 us
    pallas_call x1, Pallas kernels, finish(): pl.pallas_call(finish_kernel, grid=(NB // 2,), in_specs=[block, pl.BlockS...  10.4 us
    pallas_call x1, Pallas kernels, overlaps(): pl.pallas_call(overlap_kernel, grid=(NB,), in_specs=[pl.BlockSpec((slots,...  9.49 us
  transfers between devices with their start and end apart: 4, of which 2 were waited for; matrix products, arithmetic and copies ran while one was open for 4% of the time, Pallas kernels for 13%

profile of v1, /device:TPU:9, one launch (start us, length us, event | category | flops | bytes accessed | tf_op | source)
XLA Modules:
  0.0 205.9 jit_solution(9255656032216565754)
XLA Ops:
  0.6 0.8 copy.148
  2.9 1.2 dynamic-slice
  5.0 56.8 %all-reduce = f32[7696]{0:T(1024)S(1)} all-reduce(f32[7696]{0:T(1024)S(1)} %maximum_dynamic-update-slice_fusion), channel_id=2, replica_groups=mesh['tile'=16,'nrn'=2] {'tile'}, use_global_device_ids=true, to_apply=%add | all-reduce | flops 7696 | bytes 61568
  64.2 0.8 copy.153
  66.0 1.8 select_reduce_fusion
  69.3 0.8 slice_reduce_fusion
  70.1 14.6 %extract_windows.16 = bf16[400,16,128]{2,1,0:T(8,128)(2,1)} custom-call(s32[400]{0:T(512)} %reshape_squeeze.20.rows_ref, s32[400]{0:T(512)} %reshape_squeeze.21.cols_ref, s32[16]{0:T(128)} %get-tuple-element.554.counts_ref, s32[16]{0:T(128)} %reshape_squeeze.22.shift_ref, s32[1]{0:T(128)} %constant.279.clone.1.group_ref, bf16[8,1024,1024]{2,1,0:T(8,128)(2,1)} %bitcast.100), custom_call_target="tpu_custom_call" | custom-call | tf_op jit(solution)/shard_map/extract_windows/pallas_call | solution.py:91
  84.7 1.6 broadcast_in_dim.194
  86.3 5.8 %all-to-all-start.2 = ((bf16[400,16,128]{2,1,0:T(8,128)(2,1)}), bf16[400,16,128]{2,1,0:T(8,128)(2,1)S(1)}, u32[]{:S(2)}, u32[]{:S(2)}) async-start(bf16[400,16,128]{2,1,0:T(8,128)(2,1)} %extract_windows.16), calls=%async_computation.2 | async-start | bytes 3276800 | tf_op jit(solution)/shard_map/all_to_all | solution.py:432
  93.3 4.0 %collective-permute-start.1 = (bf16[768,128]{1,0:T(8,128)(2,1)}, bf16[768,128]{1,0:T(8,128)(2,1)S(1)}, u32[]{:S(2)}, u32[]{:S(2)}) collective-permute-start(bf16[768,128]{1,0:T(8,128)(2,1)} %bitcast.20), channel_id=1, source_target_pairs={{2,0},{4,2},{6,4},{8,6},{10,8},{12,10},{14,12},{16,14},{18,16},{20... | collective-permute-start | bytes 589832 | tf_op jit(solution)/shard_map/ppermute | solution.py:454
  97.9 1.9 collective-permute-start
  101.7 14.8 %extract_windows.17 = bf16[400,16,128]{2,1,0:T(8,128)(2,1)} custom-call(s32[400]{0:T(512)} %reshape_squeeze.23.rows_ref, s32[400]{0:T(512)} %reshape_squeeze.24.cols_ref, s32[16]{0:T(128)} %get-tuple-element.553.counts_ref, s32[16]{0:T(128)} %reshape_squeeze.22.shift_ref, s32[1]{0:T(128)} %constant.279.clone.1.group_ref, bf16[8,1024,1024]{2,1,0:T(8,128)(2,1)} %bitcast.103), custom_call_target="tpu_custom_call" | custom-call | tf_op jit(solution)/shard_map/extract_windows/pallas_call | solution.py:91
  116.5 6.6 %all-to-all-done.2.refs_0_ = bf16[400,16,128]{2,1,0:T(8,128)(2,1)S(1)} async-done(((bf16[400,16,128]{2,1,0:T(8,128)(2,1)}), bf16[400,16,128]{2,1,0:T(8,128)(2,1)S(1)}, u32[]{:S(2)}, u32[]{:S(2)}) %all-to-all-start.2) | async-done | bytes 1638432 | tf_op jit(solution)/shard_map/all_to_all | solution.py:432
  123.0 7.6 %all-to-all-start.3 = ((bf16[400,16,128]{2,1,0:T(8,128)(2,1)}), bf16[400,16,128]{2,1,0:T(8,128)(2,1)}, u32[]{:S(2)}, u32[]{:S(2)}) async-start(bf16[400,16,128]{2,1,0:T(8,128)(2,1)} %extract_windows.17), calls=%async_computation.3 | async-start | bytes 3276800 | tf_op jit(solution)/shard_map/all_to_all | solution.py:432
  131.2 1.6 window_feet.1.feet_ref
  132.7 1.1 copy-done
  134.0 0.9 copy.178
  135.3 0.9 copy.154
  138.9 1.1 pad_maximum_fusion.1.cols_ref
  140.0 9.5 %denom_c.1.denom_ref = f32[96,128]{1,0:T(8,128)S(1)} custom-call(bf16[96,2048]{1,0:T(8,128)(2,1)S(1)} %bitcast.93, s32[16,96,1]{2,1,0:T(8,128)S(1)} %copy.163.own_ids_ref, bf16[3072,128]{1,0:T(8,128)(2,1)S(1)} %pad_maximum_fusion.1.cols_ref, s32[1,3072]{1,0:T(1,128)S(1)} %bitcast.98, f32[3072,128]{1,0:T(8,128)S(1)} %pad_maximum_fusion.traces_ref), custom_call_target="tpu_custom_call" | custom-call | tf_op jit(solution)/shard_map/denom_c/pallas_call | solution.py:210
  149.5 16.1 %all-to-all-done.3.refs_1_ = bf16[400,16,128]{2,1,0:T(8,128)(2,1)} async-done(((bf16[400,16,128]{2,1,0:T(8,128)(2,1)}), bf16[400,16,128]{2,1,0:T(8,128)(2,1)}, u32[]{:S(2)}, u32[]{:S(2)}) %all-to-all-start.3) | async-done | bytes 1638432 | tf_op jit(solution)/shard_map/all_to_all | solution.py:432
  165.5 1.4 copy-done.1
  166.9 8.0 %update_traces.1 = (f32[96,128]{1,0:T(8,128)S(1)}, f32[2,768,128]{2,1,0:T(8,128)S(1)}) custom-call(s32[384]{0:T(512)S(1)} %fusion.34.index_ref, bf16[6144,128]{1,0:T(8,128)(2,1)S(1)} %copy-done.1, bf16[384,16,128]{2,1,0:T(8,128)(2,1)} %bitcast.106, f32[96,128]{1,0:T(8,128)S(1)} %copy.170.traces_ref, f32[96,128]{1,0:T(8,128)S(1)} %denom_c.1.denom_ref, ...), custom_call_target="tpu_custom_call" | custom-call | tf_op jit(solution)/shard_map/update_traces/pallas_call | solution.py:307
  174.9 0.9 copy-done.4
  176.6 13.1 %exchange.1 = (f32[5,96,128]{2,1,0:T(8,128)}, f32[1536,128]{1,0:T(8,128)}) custom-call(f32[96,128]{1,0:T(8,128)} %copy-done.7, f32[1536,128]{1,0:T(8,128)} %bitcast.95), custom_call_target="tpu_custom_call" | custom-call | tf_op jit(solution)/shard_map/exchange/pallas_call | solution.py:167
  189.7 1.0 copy-done.3
  190.7 1.1 copy-done.5
  191.8 1.1 copy-done.6
  193.0 0.8 copy-done.8
  193.8 0.9 copy-done.9
  194.7 10.4 %new_footprints.1 = bf16[96,2048]{1,0:T(8,128)(2,1)S(1)} custom-call(bf16[96,2048]{1,0:T(8,128)(2,1)S(1)} %bitcast.94, s32[16,96,1]{2,1,0:T(8,128)S(1)} %copy.163.own_ids_ref, bf16[3072,128]{1,0:T(8,128)(2,1)S(1)} %pad_maximum_fusion.1.cols_ref, s32[1,3072]{1,0:T(1,128)S(1)} %bitcast.99, f32[96,128]{1,0:T(8,128)S(1)} %copy-done.8, ...), custom_call_target="tpu_custom_call" | custom-call | tf_op jit(solution)/shard_map/new_footprints/pallas_call | solution.py:365
  205.1 0.8 copy.176
  (106 shorter events, 13.3 us)
Async XLA Ops:
  65.0 19.7 %copy-start.14 = (s32[1,8,2]{2,1,0:T(8,128)}, s32[1,8,2]{2,1,0:T(8,128)S(1)}, u32[]{:S(2)}) copy-start(s32[1,8,2]{2,1,0:T(8,128)S(1)} %copy.153) | copy-start | bytes 196
  86.3 5.8 %copy-start.12 = (bf16[96,16,128]{2,1,0:T(8,128)(2,1)S(1)}, bf16[96,16,128]{2,1,0:T(8,128)(2,1)}, u32[]{:S(2)}) copy-start(bf16[96,16,128]{2,1,0:T(8,128)(2,1)} %param.12) | copy-start | bytes 1179652
  86.3 36.8 %all-to-all-start.2 = ((bf16[400,16,128]{2,1,0:T(8,128)(2,1)}), bf16[400,16,128]{2,1,0:T(8,128)(2,1)S(1)}, u32[]{:S(2)}, u32[]{:S(2)}) async-start(bf16[400,16,128]{2,1,0:T(8,128)(2,1)} %extract_windows.16), calls=%async_computation.2 | async-start | bytes 3276800 | tf_op jit(solution)/shard_map/all_to_all | solution.py:432
  93.3 44.8 %collective-permute-start.1 = (bf16[768,128]{1,0:T(8,128)(2,1)}, bf16[768,128]{1,0:T(8,128)(2,1)S(1)}, u32[]{:S(2)}, u32[]{:S(2)}) collective-permute-start(bf16[768,128]{1,0:T(8,128)(2,1)} %bitcast.20), channel_id=1, source_target_pairs={{2,0},{4,2},{6,4},{8,6},{10,8},{12,10},{14,12},{16,14},{18,16},{20... | collective-permute-start | bytes 589832 | tf_op jit(solution)/shard_map/ppermute | solution.py:454
  97.9 40.1 %collective-permute-start = (bf16[768,128]{1,0:T(8,128)(2,1)}, bf16[768,128]{1,0:T(8,128)(2,1)}, u32[]{:S(2)}, u32[]{:S(2)}) collective-permute-start(bf16[768,128]{1,0:T(8,128)(2,1)} %bitcast.17), channel_id=1, source_target_pairs={{0,2},{2,4},{4,6},{6,8},{8,10},{10,12},{12,14},{14,16},{16,18},{18... | collective-permute-start | bytes 589832 | tf_op jit(solution)/shard_map/ppermute | solution.py:453
  123.0 42.5 %all-to-all-start.3 = ((bf16[400,16,128]{2,1,0:T(8,128)(2,1)}), bf16[400,16,128]{2,1,0:T(8,128)(2,1)}, u32[]{:S(2)}, u32[]{:S(2)}) async-start(bf16[400,16,128]{2,1,0:T(8,128)(2,1)} %extract_windows.17), calls=%async_computation.3 | async-start | bytes 3276800 | tf_op jit(solution)/shard_map/all_to_all | solution.py:432
  130.6 3.2 %copy-start.16 = (f32[1,96,4]{1,2,0:T(4,128)S(1)}, f32[1,96,4]{1,2,0:T(4,128)}, u32[]{:S(2)}) copy-start(f32[1,96,4]{1,2,0:T(4,128)} %param.14) | copy-start | bytes 4612
  130.7 4.2 %copy-start.15 = (s32[96,16]{0,1:T(8,128)S(1)}, s32[96,16]{0,1:T(8,128)}, u32[]{:S(2)}) copy-start(s32[96,16]{0,1:T(8,128)} %param.13) | copy-start | bytes 18436
  132.7 1.2 copy-start
  137.9 1.0 copy-start.11
  138.0 2.0 copy-start.2
  138.0 0.7 copy-start.13
  165.5 1.4 copy-start.1
  174.9 0.9 copy-start.4
  175.8 0.8 copy-start.7
  189.7 1.0 copy-start.3
  190.7 1.1 copy-start.5
  191.8 1.1 copy-start.6
  193.0 0.8 copy-start.8
  193.8 0.9 copy-start.9

commit v2 on v1

--- a/solution.py
+++ b/solution.py
@@ -100,82 +100,53 @@
     )(rows.reshape(-1), cols.reshape(-1), counts, shifts.reshape(-1), group.reshape(1), movie)
 
 
-def exchange_kernel(tiles, new_ref, numer_ref, near_ref, other_ref, send_sem, recv_sem):
+def gather_kernel(tiles, own_ref, all_ref, send_sem, recv_sem, own_sem):
     t, p = lax.axis_index("tile"), lax.axis_index("nrn")
-    q = 1 - p
-    has_above, has_below = t > 0, t < tiles - 1
     mesh_id = pl.DeviceIdType.MESH
     barrier = pltpu.get_barrier_semaphore()
-    pl.semaphore_signal(barrier, inc=1, device_id=(t, q), device_id_type=mesh_id)
-
-    @pl.when(has_above)
-    def _():
-        for peer in (p, q):
-            pl.semaphore_signal(barrier, inc=1, device_id=(t - 1, peer), device_id_type=mesh_id)
-
-    @pl.when(has_below)
-    def _():
-        for peer in (p, q):
-            pl.semaphore_signal(barrier, inc=1, device_id=(t + 1, peer), device_id_type=mesh_id)
-
-    pl.semaphore_wait(barrier, 1 + 2 * has_above.astype(jnp.int32) + 2 * has_below.astype(jnp.int32))
-
-    def copy(src, dst, i, to):
+
+    def peer(i):
+        return lax.rem(t + i, tiles)
+
+    @pl.loop(1, tiles)
+    def _(i):
+        pl.semaphore_signal(barrier, inc=1, device_id=(peer(i), p), device_id_type=mesh_id)
+
+    pl.semaphore_wait(barrier, tiles - 1)
+
+    def copy(i, slot):
         return pltpu.make_async_remote_copy(
-            src_ref=src, dst_ref=dst, send_sem=send_sem.at[i], recv_sem=recv_sem.at[i],
-            device_id=to, device_id_type=mesh_id,
+            src_ref=own_ref, dst_ref=all_ref.at[slot], send_sem=send_sem.at[i], recv_sem=recv_sem.at[i],
+            device_id=(peer(i), p), device_id_type=mesh_id,
         )
 
-    partner = copy(new_ref, near_ref.at[0], 0, (t, q))
-    large = copy(numer_ref, other_ref, 5, (t, q))
-    to_below = [copy(new_ref, near_ref.at[1 + i], 1 + i, (t + 1, peer)) for i, peer in enumerate((p, q))]
-    to_above = [copy(new_ref, near_ref.at[3 + i], 3 + i, (t - 1, peer)) for i, peer in enumerate((p, q))]
-
-    @pl.when(has_below)
-    def _():
-        for one in to_below:
-            one.start()
-
-    @pl.when(has_above)
-    def _():
-        for one in to_above:
-            one.start()
-
-    partner.start()
-    large.start()
-
-    @pl.when(has_below)
-    def _():
-        for one in to_below:
-            one.wait_send()
-        for one in to_above:
-            one.wait_recv()
-
-    @pl.when(has_above)
-    def _():
-        for one in to_above:
-            one.wait_send()
-        for one in to_below:
-            one.wait_recv()
-
-    partner.wait()
-    large.wait()
-
-
-def exchange(new, numer, tiles):
-    anywhere = pl.BlockSpec(memory_space=pl.ANY)
+    @pl.loop(1, tiles)
+    def _(i):
+        copy(i, t).start()
+
+    own = pltpu.make_async_copy(own_ref, all_ref.at[t], own_sem)
+    own.start()
+    own.wait()
+
+    @pl.loop(1, tiles)
+    def _(i):
+        copy(i, t).wait_send()
+        copy(i, lax.rem(t + tiles - i, tiles)).wait_recv()
+
+
+def gather(own, tiles):
+    vmem = pl.BlockSpec(memory_space=pltpu.VMEM)
     return pl.pallas_call(
-        functools.partial(exchange_kernel, tiles),
-        in_specs=[anywhere, anywhere],
-        out_specs=[anywhere, anywhere],
-        out_shape=[
-            jax.ShapeDtypeStruct((5,) + new.shape, jnp.float32),
-            jax.ShapeDtypeStruct(numer.shape, jnp.float32),
+        functools.partial(gather_kernel, tiles),
+        in_specs=[vmem],
+        out_specs=vmem,
+        out_shape=jax.ShapeDtypeStruct((tiles,) + own.shape, own.dtype),
+        scratch_shapes=[
+            pltpu.SemaphoreType.DMA((tiles,)), pltpu.SemaphoreType.DMA((tiles,)), pltpu.SemaphoreType.DMA,
         ],
-        scratch_shapes=[pltpu.SemaphoreType.DMA((6,)), pltpu.SemaphoreType.DMA((6,))],
         compiler_params=pltpu.CompilerParams(collective_id=0, has_side_effects=True),
-        name="exchange",
-    )(new, numer)
+        name="gather_numbers",
+    )(own)
 
 
 def overlap_kernel(own_ref, own_ids_ref, cols_ref, col_ids_ref, traces_ref, out_ref, acc):
@@ -327,52 +298,125 @@
 
 
 def finish_kernel(
-    own_ref, own_ids_ref, cols_ref, col_ids_ref, new_ref, near_ref, mine_ref, other_ref, out_ref, pair
+    tiles, own_ref, own_ids_ref, cols_ref, col_ids_ref, new_ref, numer_ref, out_ref,
+    near_ref, other_ref, pair, send_sem, recv_sem,
 ):
-    j = pl.program_id(0)
+    t, p = lax.axis_index("tile"), lax.axis_index("nrn")
+    q = 1 - p
+    has_above, has_below = t > 0, t < tiles - 1
+    mesh_id = pl.DeviceIdType.MESH
+    barrier = pltpu.get_barrier_semaphore()
+    pl.semaphore_signal(barrier, inc=1, device_id=(t, q), device_id_type=mesh_id)
+
+    @pl.when(has_above)
+    def _():
+        for peer in (p, q):
+            pl.semaphore_signal(barrier, inc=1, device_id=(t - 1, peer), device_id_type=mesh_id)
+
+    @pl.when(has_below)
+    def _():
+        for peer in (p, q):
+            pl.semaphore_signal(barrier, inc=1, device_id=(t + 1, peer), device_id_type=mesh_id)
+
+    pl.semaphore_wait(barrier, 1 + 2 * has_above.astype(jnp.int32) + 2 * has_below.astype(jnp.int32))
+
+    def copy(src, dst, i, to):
+        return pltpu.make_async_remote_copy(
+            src_ref=src, dst_ref=dst, send_sem=send_sem.at[i], recv_sem=recv_sem.at[i],
+            device_id=to, device_id_type=mesh_id,
+        )
+
+    partner = copy(new_ref, near_ref.at[0], 0, (t, q))
+    large = copy(numer_ref, other_ref, 5, (t, q))
+    to_below = [copy(new_ref, near_ref.at[1 + i], 1 + i, (t + 1, peer)) for i, peer in enumerate((p, q))]
+    to_above = [copy(new_ref, near_ref.at[3 + i], 3 + i, (t - 1, peer)) for i, peer in enumerate((p, q))]
+
+    @pl.when(has_below)
+    def _():
+        for one in to_below:
+            one.start()
+
+    @pl.when(has_above)
+    def _():
+        for one in to_above:
+            one.start()
+
+    partner.start()
+    large.start()
+
     slots = new_ref.shape[0]
 
-    @pl.when(j == 0)
-    def _():
-        def products(own, up, down):
-            columns = jnp.concatenate([own] * NB + [up] * (NB // 2) + [down] * (NB // 2), axis=0)
-            return lax.dot_general(
-                own, columns, (((1,), (1,)), ((), ())), precision=EXACT, preferred_element_type=jnp.float32
+    @pl.when(has_below)
+    def _():
+        for one in to_above:
+            one.wait_recv()
+
+    @pl.when(has_above)
+    def _():
+        for one in to_below:
+            one.wait_recv()
+
+    partner.wait()
+
+    def products(own, up, down):
+        columns = jnp.concatenate([own] * NB + [up] * (NB // 2) + [down] * (NB // 2), axis=0)
+        return lax.dot_general(
+            own, columns, (((1,), (1,)), ((), ())), precision=EXACT, preferred_element_type=jnp.float32
+        )
+
+    both = products(new_ref[...], near_ref[1], near_ref[3])
+    both += products(near_ref[0], near_ref[2], near_ref[4])
+    pair[...] = both * (1.0 / WIN_C)
+    large.wait()
+
+    @pl.loop(0, NB // 2)
+    def _(j):
+        highs, lows = [], []
+        for e in range(2):
+            weight = jnp.where(own_ids_ref[2 * j + e] == col_ids_ref[...], pair[...], 0.0)
+            highs.append(weight.astype(jnp.bfloat16))
+            lows.append((weight - highs[-1].astype(jnp.float32)).astype(jnp.bfloat16))
+        sums = jnp.dot(jnp.concatenate(highs + lows, axis=0), cols_ref[...], preferred_element_type=jnp.float32)
+        for e in range(2):
+            denom = sums[e * slots : (e + 1) * slots] + sums[(e + 2) * slots : (e + 3) * slots]
+            at = pl.ds(e * slots * (NB // 2) + j, slots, stride=NB // 2)
+            numer = numer_ref[at, :] + other_ref[at, :]
+            lanes = pl.ds(pl.multiple_of((2 * j + e) * VOX, VOX), VOX)
+            out_ref[:, lanes] = (own_ref[:, lanes].astype(jnp.float32) * numer / (denom + EPSILON)).astype(
+                jnp.bfloat16
             )
 
-        both = products(new_ref[...], near_ref[1], near_ref[3])
-        both += products(near_ref[0], near_ref[2], near_ref[4])
-        pair[...] = both * (1.0 / WIN_C)
-
-    highs, lows = [], []
-    for e in range(2):
-        weight = jnp.where(own_ids_ref[e] == col_ids_ref[...], pair[...], 0.0)
-        highs.append(weight.astype(jnp.bfloat16))
-        lows.append((weight - highs[-1].astype(jnp.float32)).astype(jnp.bfloat16))
-    sums = jnp.dot(jnp.concatenate(highs + lows, axis=0), cols_ref[...], preferred_element_type=jnp.float32)
-    for e in range(2):
-        denom = sums[e * slots : (e + 1) * slots] + sums[(e + 2) * slots : (e + 3) * slots]
-        at = pl.ds(e * slots * (NB // 2) + j, slots, stride=NB // 2)
-        numer = mine_ref[at, :] + other_ref[at, :]
-        lanes = pl.ds(e * VOX, VOX)
-        out_ref[:, lanes] = (own_ref[:, lanes].astype(jnp.float32) * numer / (denom + EPSILON)).astype(jnp.bfloat16)
-
-
-def finish(own, own_ids, cols, col_ids, new, near, mine, other):
-    slots = own.shape[0]
-    width = cols.shape[0]
-    block = pl.BlockSpec((slots, 2 * VOX), lambda j: (0, j))
+    @pl.when(has_below)
+    def _():
+        for one in to_below:
+            one.wait_send()
+
+    @pl.when(has_above)
+    def _():
+        for one in to_above:
+            one.wait_send()
+
+
+def finish(own, own_ids, cols, col_ids, new, numer, tiles):
+    vmem = pl.BlockSpec(memory_space=pltpu.VMEM)
+    slots, width = own.shape[0], cols.shape[0]
     return pl.pallas_call(
-        finish_kernel,
-        grid=(NB // 2,),
-        in_specs=[block, pl.BlockSpec((2, slots, 1), lambda j: (j, 0, 0))]
-        + [whole_spec(part.shape) for part in (cols, col_ids, new, near, mine, other)],
-        out_specs=block,
-        out_shape=jax.ShapeDtypeStruct((slots, NB * VOX), jnp.bfloat16),
-        scratch_shapes=[pltpu.VMEM((slots, width), jnp.float32)],
-        compiler_params=pltpu.CompilerParams(vmem_limit_bytes=48 * MIB),
+        functools.partial(finish_kernel, tiles),
+        in_specs=[vmem] * 6,
+        out_specs=vmem,
+        out_shape=jax.ShapeDtypeStruct(own.shape, jnp.bfloat16),
+        scratch_shapes=[
+            pltpu.VMEM((5,) + new.shape, jnp.float32),
+            pltpu.VMEM(numer.shape, jnp.float32),
+            pltpu.VMEM((slots, width), jnp.float32),
+            pltpu.SemaphoreType.DMA((6,)),
+            pltpu.SemaphoreType.DMA((6,)),
+        ],
+        compiler_params=pltpu.CompilerParams(
+            collective_id=1, has_side_effects=True, vmem_limit_bytes=48 * MIB
+        ),
         name="new_footprints",
-    )(own, own_ids, cols, col_ids, new, near, mine, other)
+    )(own, own_ids, cols, col_ids, new, numer)
 
 
 def shards(movie, shifts, footprints, blocks, traces, counts):
@@ -391,9 +435,12 @@
 
     own_traces = traces[0]
     numbers = jnp.concatenate([blocks[:, 0], counts]).astype(jnp.float32)
-    info = lax.all_gather(jnp.concatenate([numbers, own_traces.reshape(-1)]), "tile")
+    numbers = jnp.pad(numbers, (0, 2 * LANES - numbers.shape[0]))
+    numbers = jnp.concatenate([numbers, own_traces.reshape(-1)])
+    numbers = jnp.pad(numbers, (0, 8 * LANES - numbers.shape[0])).reshape(8, LANES)
+    info = gather(numbers, tiles).reshape(tiles, -1)
     base, live_count = info[:, :slots].astype(jnp.int32), info[:, slots : slots + 1].astype(jnp.int32)
-    all_traces = info[:, slots + 1 :].reshape(tiles, slots, fh)
+    all_traces = info[:, 2 * LANES : 2 * LANES + slots * fh].reshape(tiles, slots, fh)
     z, r, x = base // (rb * xb), (base // xb) % rb, base % xb
     live = jnp.arange(slots, dtype=jnp.int32) < live_count
     plane_ids = jnp.arange(Z, dtype=jnp.int32)
@@ -492,8 +539,7 @@
     new = new_wide[:, :: LANES // fh]
 
     numer = numer.reshape(-1, VOX)
-    near, numer_other = exchange(new_wide, numer, tiles)
-    new_footprints = finish(own_flat, own_ids, cols, col_ids, new_wide, near, numer, numer_other)
+    new_footprints = finish(own_flat, own_ids, cols, col_ids, new_wide, numer, tiles)
     return (new[None], new_footprints.reshape(slots, NB, VOX))
 
 

time: 206 us -> 158 us (0.77)
  blocking collectives: 56.8 us -> 0 us
  waiting for transfers between devices: 22.6 us -> 32.3 us
  Pallas kernels: 71.9 us -> 75.2 us
  local copies, waits for them, and re-layouts: 25.9 us -> 23 us
    unnamed x1 -> x0, blocking collectives: 56.8 us -> none
    all_to_all x2, waiting for transfers between devices: 22.6 us -> 32.3 us  [one_round(): lax.all_to_all(sent, 'tile', split_axis=0, concat_axis=0, tiled=True)]
    pallas_call x2, Pallas kernels: 23.5 us -> 28.8 us  [the longest x1 20.5 us: finish(): pl.pallas_call(functools.partial(finish_kernel, tiles), in_specs=[vmem] *...]
    unnamed x43 -> x34, local copies, waits for them, and re-layouts: 15.9 us -> 12.6 us
  transfers between devices with their start and end apart: 4 -> 4, of which waited for: 2 -> 2; matrix products, arithmetic and copies ran while one was open for 4% -> 6% of each run, Pallas kernels for 13% -> 16%
where the time goes in v2:
time: 158 us; the launch traced here: 157 us
  Pallas kernels  75.2 us (48%)
  waiting for transfers between devices  32.3 us (20%)
  local copies, waits for them, and re-layouts  23 us (15%)
  starting transfers between devices  18 us (11%)
  other arithmetic  5.99 us (4%)
  between operations  2.38 us (2%)
    all_to_all x2, waiting for transfers between devices, one_round(): lax.all_to_all(sent, 'tile', split_axis=0, concat_axis=0, tiled=True)  32.3 us
    pallas_call x2, Pallas kernels, extract(): pl.pallas_call(functools.partial(extract_kernel, cap, step, tiles, plane,...  27.3 us
    pallas_call x1, Pallas kernels, finish(): pl.pallas_call(functools.partial(finish_kernel, tiles), in_specs=[vmem] *...  20.5 us
    unnamed x34, local copies, waits for them, and re-layouts  12.6 us
    all_to_all x2, starting transfers between devices, one_round(): lax.all_to_all(sent, 'tile', split_axis=0, concat_axis=0, tiled=True)  12.1 us
    pallas_call x1, Pallas kernels, overlaps(): pl.pallas_call(overlap_kernel, grid=(NB,), in_specs=[pl.BlockSpec((slots,...  9.49 us
    pallas_call x1, Pallas kernels, gather(): pl.pallas_call(functools.partial(gather_kernel, tiles), in_specs=[vmem],...  8.35 us
    pallas_call x1, Pallas kernels, update(): pl.pallas_call(functools.partial(update_kernel, cap, groups, len(received...  7.95 us
  transfers between devices with their start and end apart: 4, of which 2 were waited for; matrix products, arithmetic and copies ran while one was open for 6% of the time, Pallas kernels for 16%

profile of v2, /device:TPU:9, one launch (start us, length us, event | category | flops | bytes accessed | tf_op | source)
XLA Modules:
  0.0 157.0 jit_solution(6864434090335947557)
XLA Ops:
  1.3 0.7 fusion.41
  2.0 0.8 copy.148
  3.6 8.3 %gather_numbers.1 = f32[16,8,128]{2,1,0:T(8,128)} custom-call(f32[8,128]{1,0:T(8,128)} %pad_bitcast_fusion.own_ref), custom_call_target="tpu_custom_call" | custom-call | tf_op jit(solution)/shard_map/gather_numbers/pallas_call | solution.py:139
  11.9 0.9 copy.181
  15.1 0.8 copy.153
  16.9 1.8 %select_reduce_fusion = (s32[16,2,25]{0,2,1:T(8,128)S(1)}, s32[16,2,25]{0,2,1:T(8,128)S(1)}) fusion(s32[16,96]{1,0:T(8,128)S(1)} %get-tuple-element.786, s32[16,2,96]{2,0,1:T(8,128)S(1)} %copy.151, s32[16,96]{1,0:T(8,128)S(1)} %get-tuple-element.785), kind=kLoop, calls=%fused_computation.39 | loop fusion | flops 382400 | bytes 30976 | tf_op jit(solution)/shard_map/reduce_sum | solution.py:472
  19.5 0.7 reshape_squeeze.21.cols_ref
  20.2 0.7 slice_reduce_fusion
  20.9 13.5 %extract_windows.16 = bf16[400,16,128]{2,1,0:T(8,128)(2,1)} custom-call(s32[400]{0:T(512)} %reshape_squeeze.20.rows_ref, s32[400]{0:T(512)} %reshape_squeeze.21.cols_ref, s32[16]{0:T(128)} %get-tuple-element.550.counts_ref, s32[16]{0:T(128)} %reshape_squeeze.22.shift_ref, s32[1]{0:T(128)} %constant.281.clone.1.group_ref, bf16[8,1024,1024]{2,1,0:T(8,128)(2,1)} %bitcast.104), custom_call_target="tpu_custom_call" | custom-call | tf_op jit(solution)/shard_map/extract_windows/pallas_call | solution.py:91
  34.4 1.6 %broadcast_in_dim.194 = bf16[96,4,16,128]{3,2,1,0:T(8,128)(2,1)} broadcast(bf16[]{:T(256)} %constant.262.clone.1), dimensions={} | broadcast | bytes 1572866 | tf_op jit(solution)/shard_map/broadcast_in_dim | solution.py:534
  35.9 7.0 %all-to-all-start.2 = ((bf16[400,16,128]{2,1,0:T(8,128)(2,1)}), bf16[400,16,128]{2,1,0:T(8,128)(2,1)S(1)}, u32[]{:S(2)}, u32[]{:S(2)}) async-start(bf16[400,16,128]{2,1,0:T(8,128)(2,1)} %extract_windows.16), calls=%async_computation.2 | async-start | bytes 3276800 | tf_op jit(solution)/shard_map/all_to_all | solution.py:479
  43.4 0.7 copy.174
  44.1 4.0 %collective-permute-start.1 = (bf16[768,128]{1,0:T(8,128)(2,1)}, bf16[768,128]{1,0:T(8,128)(2,1)S(1)}, u32[]{:S(2)}, u32[]{:S(2)}) collective-permute-start(bf16[768,128]{1,0:T(8,128)(2,1)} %bitcast.20), channel_id=1, source_target_pairs={{2,0},{4,2},{6,4},{8,6},{10,8},{12,10},{14,12},{16,14},{18,16},{20... | collective-permute-start | bytes 589832 | tf_op jit(solution)/shard_map/ppermute | solution.py:501
  48.1 0.7 copy.173
  48.8 1.9 %collective-permute-start = (bf16[768,128]{1,0:T(8,128)(2,1)}, bf16[768,128]{1,0:T(8,128)(2,1)}, u32[]{:S(2)}, u32[]{:S(2)}) collective-permute-start(bf16[768,128]{1,0:T(8,128)(2,1)} %bitcast.17), channel_id=1, source_target_pairs={{0,2},{2,4},{4,6},{6,8},{8,10},{10,12},{12,14},{14,16},{16,18},{18... | collective-permute-start | bytes 589832 | tf_op jit(solution)/shard_map/ppermute | solution.py:500
  52.5 13.9 %extract_windows.17 = bf16[400,16,128]{2,1,0:T(8,128)(2,1)} custom-call(s32[400]{0:T(512)} %reshape_squeeze.23.rows_ref, s32[400]{0:T(512)} %reshape_squeeze.24.cols_ref, s32[16]{0:T(128)} %get-tuple-element.549.counts_ref, s32[16]{0:T(128)} %reshape_squeeze.22.shift_ref, s32[1]{0:T(128)} %constant.281.clone.1.group_ref, bf16[8,1024,1024]{2,1,0:T(8,128)(2,1)} %bitcast.107), custom_call_target="tpu_custom_call" | custom-call | tf_op jit(solution)/shard_map/extract_windows/pallas_call | solution.py:91
  66.3 13.8 %all-to-all-done.2.refs_0_ = bf16[400,16,128]{2,1,0:T(8,128)(2,1)S(1)} async-done(((bf16[400,16,128]{2,1,0:T(8,128)(2,1)}), bf16[400,16,128]{2,1,0:T(8,128)(2,1)S(1)}, u32[]{:S(2)}, u32[]{:S(2)}) %all-to-all-start.2) | async-done | bytes 1638432 | tf_op jit(solution)/shard_map/all_to_all | solution.py:479
  80.2 5.1 %all-to-all-start.3 = ((bf16[400,16,128]{2,1,0:T(8,128)(2,1)}), bf16[400,16,128]{2,1,0:T(8,128)(2,1)}, u32[]{:S(2)}, u32[]{:S(2)}) async-start(bf16[400,16,128]{2,1,0:T(8,128)(2,1)} %extract_windows.17), calls=%async_computation.3 | async-start | bytes 3276800 | tf_op jit(solution)/shard_map/all_to_all | solution.py:479
  85.8 1.6 %window_feet.1.feet_ref = bf16[6144,128]{1,0:T(8,128)(2,1)S(1)} custom-call(bf16[768,256]{1,0:T(8,128)(2,1)S(1)} %reshape.262.masked_ref), custom_call_target="tpu_custom_call" | custom-call | tf_op jit(solution)/shard_map/window_feet/pallas_call | solution.py:222
  87.4 1.1 copy-done
  88.6 0.9 copy.180
  90.0 0.8 copy.154
  93.5 1.1 pad_maximum_fusion.1.cols_ref
  94.6 9.5 %denom_c.1.denom_ref = f32[96,128]{1,0:T(8,128)S(1)} custom-call(bf16[96,2048]{1,0:T(8,128)(2,1)S(1)} %bitcast.98, s32[16,96,1]{2,1,0:T(8,128)S(1)} %copy.163.own_ids_ref, bf16[3072,128]{1,0:T(8,128)(2,1)S(1)} %pad_maximum_fusion.1.cols_ref, s32[1,3072]{1,0:T(1,128)S(1)} %bitcast.102, f32[3072,128]{1,0:T(8,128)S(1)} %pad_maximum_fusion.traces_ref), custom_call_target="tpu_custom_call" | custom-call | tf_op jit(solution)/shard_map/denom_c/pallas_call | solution.py:181
  104.1 18.5 %all-to-all-done.3.refs_1_ = bf16[400,16,128]{2,1,0:T(8,128)(2,1)} async-done(((bf16[400,16,128]{2,1,0:T(8,128)(2,1)}), bf16[400,16,128]{2,1,0:T(8,128)(2,1)}, u32[]{:S(2)}, u32[]{:S(2)}) %all-to-all-start.3) | async-done | bytes 1638432 | tf_op jit(solution)/shard_map/all_to_all | solution.py:479
  122.6 1.4 copy-done.1
  124.0 8.0 %update_traces.1 = (f32[96,128]{1,0:T(8,128)S(1)}, f32[2,768,128]{2,1,0:T(8,128)S(1)}) custom-call(s32[384]{0:T(512)S(1)} %fusion.34.index_ref, bf16[6144,128]{1,0:T(8,128)(2,1)S(1)} %copy-done.1, bf16[384,16,128]{2,1,0:T(8,128)(2,1)} %bitcast.110, f32[96,128]{1,0:T(8,128)S(1)} %copy.170.traces_ref, f32[96,128]{1,0:T(8,128)S(1)} %denom_c.1.denom_ref, ...), custom_call_target="tpu_custom_call" | custom-call | tf_op jit(solution)/shard_map/update_traces/pallas_call | solution.py:278
  132.0 0.9 copy-done.4
  133.6 1.0 copy-done.3
  134.6 1.1 copy-done.5
  135.7 20.5 %new_footprints.1 = bf16[96,2048]{1,0:T(8,128)(2,1)S(1)} custom-call(bf16[96,2048]{1,0:T(8,128)(2,1)S(1)} %bitcast.99, s32[16,96,1]{2,1,0:T(8,128)S(1)} %copy.163.own_ids_ref, bf16[3072,128]{1,0:T(8,128)(2,1)S(1)} %pad_maximum_fusion.1.cols_ref, s32[1,3072]{1,0:T(1,128)S(1)} %bitcast.103, f32[96,128]{1,0:T(8,128)S(1)} %get-tuple-element.362.new_ref, ...), custom_call_target="tpu_custom_call" | custom-call | tf_op jit(solution)/shard_map/new_footprints/pallas_call | solution.py:403
  156.2 0.8 copy.177
  (96 shorter events, 10.8 us)
Async XLA Ops:
  15.8 18.5 %copy-start.10 = (s32[1,8,2]{2,1,0:T(8,128)}, s32[1,8,2]{2,1,0:T(8,128)S(1)}, u32[]{:S(2)}) copy-start(s32[1,8,2]{2,1,0:T(8,128)S(1)} %copy.153) | copy-start | bytes 196
  35.9 7.0 %copy-start.8 = (bf16[96,16,128]{2,1,0:T(8,128)(2,1)S(1)}, bf16[96,16,128]{2,1,0:T(8,128)(2,1)}, u32[]{:S(2)}) copy-start(bf16[96,16,128]{2,1,0:T(8,128)(2,1)} %param.12) | copy-start | bytes 1179652
  35.9 44.2 %all-to-all-start.2 = ((bf16[400,16,128]{2,1,0:T(8,128)(2,1)}), bf16[400,16,128]{2,1,0:T(8,128)(2,1)S(1)}, u32[]{:S(2)}, u32[]{:S(2)}) async-start(bf16[400,16,128]{2,1,0:T(8,128)(2,1)} %extract_windows.16), calls=%async_computation.2 | async-start | bytes 3276800 | tf_op jit(solution)/shard_map/all_to_all | solution.py:479
  44.1 48.5 %collective-permute-start.1 = (bf16[768,128]{1,0:T(8,128)(2,1)}, bf16[768,128]{1,0:T(8,128)(2,1)S(1)}, u32[]{:S(2)}, u32[]{:S(2)}) collective-permute-start(bf16[768,128]{1,0:T(8,128)(2,1)} %bitcast.20), channel_id=1, source_target_pairs={{2,0},{4,2},{6,4},{8,6},{10,8},{12,10},{14,12},{16,14},{18,16},{20... | collective-permute-start | bytes 589832 | tf_op jit(solution)/shard_map/ppermute | solution.py:501
  48.8 43.9 %collective-permute-start = (bf16[768,128]{1,0:T(8,128)(2,1)}, bf16[768,128]{1,0:T(8,128)(2,1)}, u32[]{:S(2)}, u32[]{:S(2)}) collective-permute-start(bf16[768,128]{1,0:T(8,128)(2,1)} %bitcast.17), channel_id=1, source_target_pairs={{0,2},{2,4},{4,6},{6,8},{8,10},{10,12},{12,14},{14,16},{16,18},{18... | collective-permute-start | bytes 589832 | tf_op jit(solution)/shard_map/ppermute | solution.py:500
  80.2 42.4 %all-to-all-start.3 = ((bf16[400,16,128]{2,1,0:T(8,128)(2,1)}), bf16[400,16,128]{2,1,0:T(8,128)(2,1)}, u32[]{:S(2)}, u32[]{:S(2)}) async-start(bf16[400,16,128]{2,1,0:T(8,128)(2,1)} %extract_windows.17), calls=%async_computation.3 | async-start | bytes 3276800 | tf_op jit(solution)/shard_map/all_to_all | solution.py:479
  85.3 3.2 %copy-start.12 = (f32[1,96,4]{1,2,0:T(4,128)S(1)}, f32[1,96,4]{1,2,0:T(4,128)}, u32[]{:S(2)}) copy-start(f32[1,96,4]{1,2,0:T(4,128)} %param.14) | copy-start | bytes 4612
  85.3 4.2 %copy-start.11 = (s32[96,16]{0,1:T(8,128)S(1)}, s32[96,16]{0,1:T(8,128)}, u32[]{:S(2)}) copy-start(s32[96,16]{0,1:T(8,128)} %param.13) | copy-start | bytes 18436
  87.3 1.2 copy-start
  92.5 1.0 copy-start.7
  92.6 2.0 %copy-start.2 = (bf16[12,8,16,128]{3,1,2,0:T(8,128)(2,1)S(1)}, bf16[12,8,16,128]{3,1,2,0:T(8,128)(2,1)}, u32[]{:S(2)}) copy-start(bf16[12,8,16,128]{3,1,2,0:T(8,128)(2,1)} %copy.180) | copy-start | bytes 1179652
  92.6 0.7 copy-start.9
  122.6 1.4 copy-start.1
  132.0 0.9 copy-start.4
  133.6 1.0 copy-start.3
  134.6 1.1 copy-start.5

commit v3 on v2

--- a/solution.py
+++ b/solution.py
@@ -23,7 +23,7 @@
 
 def extract_kernel(
     cap, step, tiles, plane, frames, height, width,
-    rows_ref, cols_ref, counts_ref, shift_ref, group_ref, movie_ref, out_ref, scr,
+    starts_ref, counts_ref, shift_ref, group_ref, movie_ref, out_ref, scr,
 ):
     frame = pl.program_id(0)
 
@@ -48,9 +48,10 @@
             (shift_ref[2 * (plane * frames + f)], shift_ref[2 * (plane * frames + f) + 1]) for f in range(frames)
         ]
 
-        def one(slot):
-            r0 = rows_ref[slot]
-            c0 = cols_ref[slot]
+        def one(t, slot):
+            start = starts_ref[t, plane * cap + slot]
+            r0 = start // width
+            c0 = start % width
             window = jnp.zeros((WIN_R, LANES), jnp.float32)
             for f in range(frames):
                 down, right = moves[f]
@@ -76,28 +77,28 @@
         @pl.loop(0, tiles)
         def _(t):
             def some(i, carry):
-                slots = [t * cap + i * step + j for j in range(step)]
-                windows = [one(slot) for slot in slots]
+                slots = [i * step + j for j in range(step)]
+                windows = [one(t, slot) for slot in slots]
                 for slot, window in zip(slots, windows):
-                    out_ref[slot] = window
+                    out_ref[t * cap + slot] = window
                 return carry
 
-            lax.fori_loop(0, (counts_ref[t] + step - 1) // step, some, 0)
-
-
-def extract(movie, shifts, rows, cols, counts, group, cap, step, tiles, plane, frames):
+            lax.fori_loop(0, (counts_ref[t, plane] + step - 1) // step, some, 0)
+
+
+def extract(movie, shifts, starts, counts, group, cap, step, tiles, plane, frames):
     _, height, width = movie.shape
     smem = pl.BlockSpec(memory_space=pltpu.SMEM)
     return pl.pallas_call(
         functools.partial(extract_kernel, cap, step, tiles, plane, frames, height, width),
         grid=(frames,),
-        in_specs=[smem] * 5 + [pl.BlockSpec((1, height, width), lambda f: (plane * frames + f, 0, 0))],
+        in_specs=[smem] * 4 + [pl.BlockSpec((1, height, width), lambda f: (plane * frames + f, 0, 0))],
         out_specs=pl.BlockSpec((tiles * cap, WIN_R, LANES), lambda f: (0, 0, 0)),
         out_shape=jax.ShapeDtypeStruct((tiles * cap, WIN_R, LANES), jnp.bfloat16),
         scratch_shapes=[pltpu.VMEM((frames, height + 24, width + 256), jnp.float32)],
         compiler_params=pltpu.CompilerParams(vmem_limit_bytes=56 * MIB),
         name="extract_windows",
-    )(rows.reshape(-1), cols.reshape(-1), counts, shifts.reshape(-1), group.reshape(1), movie)
+    )(starts, counts, shifts.reshape(-1), group.reshape(1), movie)
 
 
 def gather_kernel(tiles, own_ref, all_ref, send_sem, recv_sem, own_sem):
@@ -298,9 +299,13 @@
 
 
 def finish_kernel(
-    tiles, own_ref, own_ids_ref, cols_ref, col_ids_ref, new_ref, numer_ref, out_ref,
-    near_ref, other_ref, pair, send_sem, recv_sem,
+    tiles, own_in, own_ids_in, cols_in, col_ids_in, new_ref, numer_ref, out_ref,
+    own_ref, own_ids_ref, cols_ref, col_ids_ref, near_ref, other_ref, pair, send_sem, recv_sem, load_sem,
 ):
+    operands = ((own_in, own_ref), (own_ids_in, own_ids_ref), (cols_in, cols_ref), (col_ids_in, col_ids_ref))
+    loads = [pltpu.make_async_copy(src, dst, load_sem.at[i]) for i, (src, dst) in enumerate(operands)]
+    for load in loads:
+        load.start()
     t, p = lax.axis_index("tile"), lax.axis_index("nrn")
     q = 1 - p
     has_above, has_below = t > 0, t < tiles - 1
@@ -358,15 +363,20 @@
 
     partner.wait()
 
-    def products(own, up, down):
-        columns = jnp.concatenate([own] * NB + [up] * (NB // 2) + [down] * (NB // 2), axis=0)
-        return lax.dot_general(
-            own, columns, (((1,), (1,)), ((), ())), precision=EXACT, preferred_element_type=jnp.float32
-        )
-
-    both = products(new_ref[...], near_ref[1], near_ref[3])
-    both += products(near_ref[0], near_ref[2], near_ref[4])
-    pair[...] = both * (1.0 / WIN_C)
+    def all_frames(mine, other):
+        lane = lax.broadcasted_iota(jnp.int32, mine.shape, 1)
+        return jnp.where((lane & 1) == p, mine, other)
+
+    own = all_frames(new_ref[...], near_ref[0])
+    up = all_frames(near_ref[1], near_ref[2])
+    down = all_frames(near_ref[3], near_ref[4])
+    columns = jnp.concatenate([own] * NB + [up] * (NB // 2) + [down] * (NB // 2), axis=0)
+    both = lax.dot_general(
+        own, columns, (((1,), (1,)), ((), ())), precision=EXACT, preferred_element_type=jnp.float32
+    )
+    pair[...] = both * (2.0 / WIN_C)
+    for load in loads:
+        load.wait()
     large.wait()
 
     @pl.loop(0, NB // 2)
@@ -402,15 +412,17 @@
     slots, width = own.shape[0], cols.shape[0]
     return pl.pallas_call(
         functools.partial(finish_kernel, tiles),
-        in_specs=[vmem] * 6,
+        in_specs=[pl.BlockSpec(memory_space=pl.ANY)] * 4 + [vmem] * 2,
         out_specs=vmem,
         out_shape=jax.ShapeDtypeStruct(own.shape, jnp.bfloat16),
-        scratch_shapes=[
+        scratch_shapes=[pltpu.VMEM(part.shape, part.dtype) for part in (own, own_ids, cols, col_ids)]
+        + [
             pltpu.VMEM((5,) + new.shape, jnp.float32),
             pltpu.VMEM(numer.shape, jnp.float32),
             pltpu.VMEM((slots, width), jnp.float32),
             pltpu.SemaphoreType.DMA((6,)),
             pltpu.SemaphoreType.DMA((6,)),
+            pltpu.SemaphoreType.DMA((4,)),
         ],
         compiler_params=pltpu.CompilerParams(
             collective_id=1, has_side_effects=True, vmem_limit_bytes=48 * MIB
@@ -455,8 +467,7 @@
     first_plane = (me // groups) * planes
     my_place = lax.dynamic_slice_in_dim(jnp.where(cover, rank, -1), first_plane, planes, 1)
     my_totals = lax.dynamic_slice_in_dim(totals, first_plane, planes, 1)
-    row_start = jnp.arange(tiles, dtype=jnp.int32)[:, None] * band + PR * r
-    col_start = PC * x
+    pixel_start = (jnp.arange(tiles, dtype=jnp.int32)[:, None] * band + PR * r) * width + PC * x
     own_z = blocks[:, 0] // (rb * xb)
     own_live = jnp.arange(slots, dtype=jnp.int32) < counts[0]
     own_plane = own_z[:, None] + jnp.arange(SPAN, dtype=jnp.int32)
@@ -468,13 +479,12 @@
         offset = number * cap
         slot_ids = jnp.arange(cap, dtype=jnp.int32) + offset
         hit = my_place[:, :, None] == slot_ids[:, None]
-        rows = jnp.where(hit, row_start[:, None, None, :], 0).sum(axis=3)
-        cols = jnp.where(hit, col_start[:, None, None, :], 0).sum(axis=3)
+        starts = jnp.where(hit, pixel_start[:, None, None, :], 0).sum(axis=3).reshape(tiles, planes * cap)
         limits = jnp.clip(my_totals - offset, 0, cap)
         received = []
         for d in range(planes):
             sent = extract(
-                movie[0], shifts[0], rows[:, d], cols[:, d], limits[:, d], me % groups, cap, step, tiles, d, frames
+                movie[0], shifts[0], starts, limits, me % groups, cap, step, tiles, d, frames
             )
             received.append(lax.all_to_all(sent, "tile", split_axis=0, concat_axis=0, tiled=True))
         local = own_place - offset
@@ -528,10 +538,11 @@
     feet = window_feet(pair_feet)
     received, index, valid = one_round(0)
     index = jnp.where(valid, index + (own_plane % planes) * (tiles * cap), -1).reshape(-1)
+    zero, denom_c = lax.optimization_barrier((jnp.zeros((1, 1, 1, 1), jnp.bfloat16), denom_c))
     _, later = lax.while_loop(
         lambda state: state[0] < rounds,
         later_round,
-        (jnp.int32(1), jnp.zeros((slots, SPAN, WIN_R, LANES), jnp.bfloat16)),
+        (jnp.int32(1), jnp.broadcast_to(zero, (slots, SPAN, WIN_R, LANES))),
     )
     new_wide, numer = update(
         index, feet, later.reshape(-1, WIN_R, LANES), wide(own_traces), denom_c, received, cap, groups

time: 158 us -> 176 us (1.11)
  waiting for transfers between devices: 32.3 us -> 53.6 us
  local copies, waits for them, and re-layouts: 23 us -> 18.4 us
  Pallas kernels: 75.2 us -> 77.5 us
    all_to_all x2, waiting for transfers between devices: 32.3 us -> 53.6 us  [one_round(): lax.all_to_all(sent, 'tile', split_axis=0, concat_axis=0, tiled=True)]
    unnamed x34 -> x37, local copies, waits for them, and re-layouts: 12.6 us -> 9.28 us
    another operation x4 -> x0, local copies, waits for them, and re-layouts: 2.7 us -> none  [the longest x2 1.36 us: extract(): cols.reshape(-1)]
    pallas_call x2, Pallas kernels: 27.3 us -> 29.7 us  [extract(): pl.pallas_call(functools.partial(extract_kernel, cap, step, tiles, plane,...]
  transfers between devices with their start and end apart: 4 -> 4, of which waited for: 2 -> 2; matrix products, arithmetic and copies ran while one was open for 6% -> 7% of each run, Pallas kernels for 16% -> 22%
where the time goes in v3:
time: 176 us
  Pallas kernels  77.5 us (44%)
  waiting for transfers between devices  53.6 us (30%)
  starting transfers between devices  18.7 us (11%)
  local copies, waits for them, and re-layouts  18.4 us (10%)
  other arithmetic  5.03 us (3%)
  between operations  2.52 us (1%)
    all_to_all x2, waiting for transfers between devices, one_round(): lax.all_to_all(sent, 'tile', split_axis=0, concat_axis=0, tiled=True)  53.6 us
    pallas_call x2, Pallas kernels, extract(): pl.pallas_call(functools.partial(extract_kernel, cap, step, tiles, plane,...  29.7 us
    pallas_call x1, Pallas kernels, finish(): pl.pallas_call(functools.partial(finish_kernel, tiles), in_specs=[pl.Bloc...  20.9 us
    all_to_all x2, starting transfers between devices, one_round(): lax.all_to_all(sent, 'tile', split_axis=0, concat_axis=0, tiled=True)  11.6 us
    pallas_call x1, Pallas kernels, overlaps(): pl.pallas_call(overlap_kernel, grid=(NB,), in_specs=[pl.BlockSpec((slots,...  9.49 us
    unnamed x37, local copies, waits for them, and re-layouts  9.28 us
    pallas_call x1, Pallas kernels, gather(): pl.pallas_call(functools.partial(gather_kernel, tiles), in_specs=[vmem],...  7.97 us
    pallas_call x1, Pallas kernels, update(): pl.pallas_call(functools.partial(update_kernel, cap, groups, len(received...  7.95 us
  transfers between devices with their start and end apart: 4, of which 2 were waited for; matrix products, arithmetic and copies ran while one was open for 7% of the time, Pallas kernels for 22%

profile of v3, /device:TPU:9, one launch (start us, length us, event | category | flops | bytes accessed | tf_op | source)
XLA Modules:
  0.0 175.9 jit_solution(1829041246306066584)
XLA Ops:
  1.4 1.2 broadcast_select_fusion
  2.9 3.1 %collective-permute-start = (bf16[768,128]{1,0:T(8,128)(2,1)S(1)}, bf16[768,128]{1,0:T(8,128)(2,1)S(1)}, u32[]{:S(2)}, u32[]{:S(2)}) collective-permute-start(bf16[768,128]{1,0:T(8,128)(2,1)S(1)} %bitcast.105), channel_id=1, source_target_pairs={{0,2},{2,4},{4,6},{6,8},{8,10},{10,12},{12,14},{14,16},{16,18},{18... | collective-permute-start | bytes 589832 | tf_op jit(solution)/shard_map/ppermute | solution.py:510
  6.0 4.0 %collective-permute-start.1 = (bf16[768,128]{1,0:T(8,128)(2,1)S(1)}, bf16[768,128]{1,0:T(8,128)(2,1)S(1)}, u32[]{:S(2)}, u32[]{:S(2)}) collective-permute-start(bf16[768,128]{1,0:T(8,128)(2,1)S(1)} %bitcast.106), channel_id=1, source_target_pairs={{2,0},{4,2},{6,4},{8,6},{10,8},{12,10},{14,12},{16,14},{18,16},{20... | collective-permute-start | bytes 589832 | tf_op jit(solution)/shard_map/ppermute | solution.py:511
  10.4 0.6 pad_bitcast_fusion.own_ref
  11.0 8.0 %gather_numbers.1 = f32[16,8,128]{2,1,0:T(8,128)} custom-call(f32[8,128]{1,0:T(8,128)} %pad_bitcast_fusion.own_ref), custom_call_target="tpu_custom_call" | custom-call | tf_op jit(solution)/shard_map/gather_numbers/pallas_call | solution.py:140
  19.0 0.9 copy.108
  20.7 0.6 reduce_max.9
  22.5 0.6 reshape_squeeze.8.shift_ref
  25.3 0.7 broadcast_clamp_fusion
  26.0 0.7 dynamic-slice_bitcast_fusion
  26.9 0.9 select_reduce_fusion.1
  27.9 0.7 reshape.273.starts_ref
  28.8 14.9 %extract_windows.16 = bf16[400,16,128]{2,1,0:T(8,128)(2,1)} custom-call(s32[16,50]{1,0:T(8,128)} %reshape.273.starts_ref, s32[16,2]{1,0:T(8,128)} %get-tuple-element.504.counts_ref, s32[16]{0:T(128)} %reshape_squeeze.8.shift_ref, s32[1]{0:T(128)} %constant.284.clone.1.group_ref, bf16[8,1024,1024]{2,1,0:T(8,128)(2,1)} %bitcast.82), custom_call_target="tpu_custom_call" | custom-call | tf_op jit(solution)/shard_map/extract_windows/pallas_call | solution.py:92
  43.9 9.5 %denom_c.1.denom_ref = f32[96,128]{1,0:T(8,128)S(1)} custom-call(bf16[96,2048]{1,0:T(8,128)(2,1)S(1)} %bitcast.76, s32[16,96,1]{2,1,0:T(8,128)S(1)} %copy.91.own_ids_ref.own_ids_in, bf16[3072,128]{1,0:T(8,128)(2,1)S(1)} %pad_maximum_fusion.1.cols_ref.cols_in, s32[1,3072]{1,0:T(1,128)S(1)} %bitcast.80, f32[3072,128]{1,0:T(8,128)S(1)} %pad_maximum_fusion.traces_ref), custom_call_target="tpu_custom_call" | custom-call | tf_op jit(solution)/shard_map/denom_c/pallas_call | solution.py:182
  53.4 1.5 broadcast_in_dim.187
  54.9 6.5 %all-to-all-start.2 = ((bf16[400,16,128]{2,1,0:T(8,128)(2,1)}), bf16[400,16,128]{2,1,0:T(8,128)(2,1)S(1)}, u32[]{:S(2)}, u32[]{:S(2)}) async-start(bf16[400,16,128]{2,1,0:T(8,128)(2,1)} %extract_windows.16), calls=%async_computation.2 | async-start | bytes 3276800 | tf_op jit(solution)/shard_map/all_to_all | solution.py:489
  61.4 14.8 %extract_windows.17 = bf16[400,16,128]{2,1,0:T(8,128)(2,1)} custom-call(s32[16,50]{1,0:T(8,128)} %reshape.273.starts_ref, s32[16,2]{1,0:T(8,128)} %get-tuple-element.504.counts_ref, s32[16]{0:T(128)} %reshape_squeeze.8.shift_ref, s32[1]{0:T(128)} %constant.284.clone.1.group_ref, bf16[8,1024,1024]{2,1,0:T(8,128)(2,1)} %bitcast.85), custom_call_target="tpu_custom_call" | custom-call | tf_op jit(solution)/shard_map/extract_windows/pallas_call | solution.py:92
  76.2 22.4 %all-to-all-done.2.refs_0_ = bf16[400,16,128]{2,1,0:T(8,128)(2,1)S(1)} async-done(((bf16[400,16,128]{2,1,0:T(8,128)(2,1)}), bf16[400,16,128]{2,1,0:T(8,128)(2,1)S(1)}, u32[]{:S(2)}, u32[]{:S(2)}) %all-to-all-start.2) | async-done | bytes 1638432 | tf_op jit(solution)/shard_map/all_to_all | solution.py:489
  98.6 5.1 %all-to-all-start.3 = ((bf16[400,16,128]{2,1,0:T(8,128)(2,1)}), bf16[400,16,128]{2,1,0:T(8,128)(2,1)}, u32[]{:S(2)}, u32[]{:S(2)}) async-start(bf16[400,16,128]{2,1,0:T(8,128)(2,1)} %extract_windows.17), calls=%async_computation.3 | async-start | bytes 3276800 | tf_op jit(solution)/shard_map/all_to_all | solution.py:489
  103.8 1.9 %reshape.264.masked_ref = bf16[768,256]{1,0:T(8,128)(2,1)} reshape(bf16[96,16,128]{2,1,0:T(8,128)(2,1)} %copy-done.8) | data formatting | bytes 786432 | tf_op jit(solution)/shard_map/reshape | solution.py:537
  106.2 1.0 copy-done.4
  107.2 1.6 window_feet.1.feet_ref
  108.7 1.2 copy-done
  109.9 31.1 %all-to-all-done.3.refs_1_ = bf16[400,16,128]{2,1,0:T(8,128)(2,1)} async-done(((bf16[400,16,128]{2,1,0:T(8,128)(2,1)}), bf16[400,16,128]{2,1,0:T(8,128)(2,1)}, u32[]{:S(2)}, u32[]{:S(2)}) %all-to-all-start.3) | async-done | bytes 1638432 | tf_op jit(solution)/shard_map/all_to_all | solution.py:489
  141.0 1.4 copy-done.1
  142.5 8.0 %update_traces.1 = (f32[96,128]{1,0:T(8,128)S(1)}, f32[2,768,128]{2,1,0:T(8,128)S(1)}) custom-call(s32[384]{0:T(512)S(1)} %fusion.33.index_ref, bf16[6144,128]{1,0:T(8,128)(2,1)S(1)} %copy-done.1, bf16[384,16,128]{2,1,0:T(8,128)(2,1)} %bitcast.88, f32[96,128]{1,0:T(8,128)S(1)} %copy.85.traces_ref, f32[96,128]{1,0:T(8,128)S(1)} %denom_c.1.denom_ref, ...), custom_call_target="tpu_custom_call" | custom-call | tf_op jit(solution)/shard_map/update_traces/pallas_call | solution.py:279
  150.4 0.9 copy-done.5
  151.4 1.0 copy-done.3
  152.4 1.1 copy-done.6
  153.6 20.9 %new_footprints.1 = bf16[96,2048]{1,0:T(8,128)(2,1)S(1)} custom-call(bf16[96,2048]{1,0:T(8,128)(2,1)S(1)} %bitcast.77, s32[16,96,1]{2,1,0:T(8,128)S(1)} %copy.91.own_ids_ref.own_ids_in, bf16[3072,128]{1,0:T(8,128)(2,1)S(1)} %pad_maximum_fusion.1.cols_ref.cols_in, s32[1,3072]{1,0:T(1,128)S(1)} %bitcast.81, f32[96,128]{1,0:T(8,128)S(1)} %get-tuple-element.346.new_ref, ...), custom_call_target="tpu_custom_call" | custom-call | tf_op jit(solution)/shard_map/new_footprints/pallas_call | solution.py:413
  174.4 0.8 copy.104
  175.2 0.7 copy.99
  (91 shorter events, 5.3 us)
Async XLA Ops:
  0.6 19.2 %copy-start.9 = (bf16[96,16,128]{2,1,0:T(8,128)(2,1)S(1)}, bf16[96,16,128]{2,1,0:T(8,128)(2,1)}, u32[]{:S(2)}) copy-start(bf16[96,16,128]{2,1,0:T(8,128)(2,1)} %param.12) | copy-start | bytes 1179652
  0.6 9.4 %copy-start.11 = (s32[96,16]{0,1:T(8,128)S(1)}, s32[96,16]{0,1:T(8,128)}, u32[]{:S(2)}) copy-start(s32[96,16]{0,1:T(8,128)} %param.13) | copy-start | bytes 18436
  0.7 9.5 %copy-start.12 = (f32[1,96,4]{1,2,0:T(4,128)S(1)}, f32[1,96,4]{1,2,0:T(4,128)}, u32[]{:S(2)}) copy-start(f32[1,96,4]{1,2,0:T(4,128)} %param.14) | copy-start | bytes 4612
  2.5 22.3 %copy-start.8 = (bf16[96,16,128]{2,1,0:T(8,128)(2,1)}, bf16[96,16,128]{2,1,0:T(8,128)(2,1)S(1)}, u32[]{:S(2)}) copy-start(bf16[96,16,128]{2,1,0:T(8,128)(2,1)S(1)} %broadcast_select_fusion) | copy-start | bytes 1179652
  2.6 19.8 %copy-start.14 = (s32[1,8,2]{1,2,0:T(2,128)S(1)}, s32[1,8,2]{1,2,0:T(2,128)}, u32[]{:S(2)}) copy-start(s32[1,8,2]{1,2,0:T(2,128)} %param.11) | copy-start | bytes 196
  2.9 40.9 %collective-permute-start = (bf16[768,128]{1,0:T(8,128)(2,1)S(1)}, bf16[768,128]{1,0:T(8,128)(2,1)S(1)}, u32[]{:S(2)}, u32[]{:S(2)}) collective-permute-start(bf16[768,128]{1,0:T(8,128)(2,1)S(1)} %bitcast.105), channel_id=1, source_target_pairs={{0,2},{2,4},{4,6},{6,8},{8,10},{10,12},{12,14},{14,16},{16,18},{18... | collective-permute-start | bytes 589832 | tf_op jit(solution)/shard_map/ppermute | solution.py:510
  6.0 37.7 %collective-permute-start.1 = (bf16[768,128]{1,0:T(8,128)(2,1)S(1)}, bf16[768,128]{1,0:T(8,128)(2,1)S(1)}, u32[]{:S(2)}, u32[]{:S(2)}) collective-permute-start(bf16[768,128]{1,0:T(8,128)(2,1)S(1)} %bitcast.106), channel_id=1, source_target_pairs={{2,0},{4,2},{6,4},{8,6},{10,8},{12,10},{14,12},{16,14},{18,16},{20... | collective-permute-start | bytes 589832 | tf_op jit(solution)/shard_map/ppermute | solution.py:511
  22.3 3.7 %copy-start.13 = (s32[16,32,96]{2,1,0:T(8,128)}, s32[16,32,96]{2,1,0:T(8,128)S(1)}, u32[]{:S(2)}) copy-start(s32[16,32,96]{2,1,0:T(8,128)S(1)} %convolution_convert_fusion) | copy-start | bytes 589828
  22.4 2.5 %copy-start.10 = (s32[1,8,2]{2,1,0:T(8,128)}, s32[1,8,2]{2,1,0:T(8,128)S(1)}, u32[]{:S(2)}) copy-start(s32[1,8,2]{2,1,0:T(8,128)S(1)} %copy.93) | copy-start | bytes 196
  25.0 18.9 %copy-start.2 = (bf16[12,8,16,128]{3,1,2,0:T(8,128)(2,1)}, bf16[12,8,16,128]{3,1,2,0:T(8,128)(2,1)S(1)}, u32[]{:S(2)}) copy-start(bf16[12,8,16,128]{3,1,2,0:T(8,128)(2,1)S(1)} %copy.107) | copy-start | bytes 1179652
  54.9 43.7 %all-to-all-start.2 = ((bf16[400,16,128]{2,1,0:T(8,128)(2,1)}), bf16[400,16,128]{2,1,0:T(8,128)(2,1)S(1)}, u32[]{:S(2)}, u32[]{:S(2)}) async-start(bf16[400,16,128]{2,1,0:T(8,128)(2,1)} %extract_windows.16), calls=%async_computation.2 | async-start | bytes 3276800 | tf_op jit(solution)/shard_map/all_to_all | solution.py:489
  98.6 42.4 %all-to-all-start.3 = ((bf16[400,16,128]{2,1,0:T(8,128)(2,1)}), bf16[400,16,128]{2,1,0:T(8,128)(2,1)}, u32[]{:S(2)}, u32[]{:S(2)}) async-start(bf16[400,16,128]{2,1,0:T(8,128)(2,1)} %extract_windows.17), calls=%async_computation.3 | async-start | bytes 3276800 | tf_op jit(solution)/shard_map/all_to_all | solution.py:489
  106.2 1.0 copy-start.4
  108.7 1.2 copy-start
  141.0 1.4 copy-start.1
  150.4 0.9 copy-start.5
  151.4 1.0 copy-start.3
  152.4 1.1 copy-start.6
